TPU v7x, 256 devices: a whole 4x4x8 slice. The times are simulated.
256 devices in a mesh: gx: 16 (over y, x), gy: 16 (over z, core).
Axes of the slice: x: 4, y: 4, z: 8, core: 2. Of those that a mesh axis runs over, the one named last changes fastest.
Arguments:
- load: float32 [3, 256, 256, 128], P(None, 'gx', 'gy'), may hold values from -8 to 8
- modulus: float32 [256, 256, 128], P('gx', 'gy'), may hold values from 0.5 to 5
- anchor: float32 [256, 256, 128], P('gx', 'gy'), may hold values from 0.05 to 0.5
- wall_mask: int32 [64, 64, 16], P('gx', 'gy'), may hold values 0 or 1
Outputs:
- solution: float32 [3, 256, 256, 128], P(None, 'gx', 'gy')
- remainder: float32 [3, 256, 256, 128], P(None, 'gx', 'gy')
All inputs are finite; a program needn't handle non-finite values. No bound on the sum of `wall_mask` on one device may be relied on, other than what follows from the above.
Results may differ from a plain program's by a relative error of at most 0.00027.
Values sent between devices are 32-bit elements; how exact they have to be, the bound alone decides.
A program may use at most 128 MiB of HBM per device.

v0:
```python
import jax
import jax.numpy as jnp
from jax import lax
from jax.sharding import PartitionSpec as P

SMOOTH = 3
COARSE_STEPS = 8


def with_halo(cells, sides, width):
    for axis, dim in sides:
        count = lax.axis_size(axis)
        ends = count - 1
        head = lax.slice_in_dim(cells, 0, width, axis=dim)
        tail = lax.slice_in_dim(cells, cells.shape[dim] - width, cells.shape[dim], axis=dim)
        cells = jnp.concatenate(
            [
                lax.ppermute(tail, axis, [(i, (i + 1) % count) for i in range(ends)]),
                cells,
                lax.ppermute(head, axis, [((i + 1) % count, i) for i in range(ends)]),
            ],
            axis=dim,
        )
    return cells


def stencil(padded, field, stiff, shift):
    beside = padded[:, 2:, 1:-1] + padded[:, :-2, 1:-1]
    beside = beside + padded[:, 1:-1, 2:] + padded[:, 1:-1, :-2]
    zpad = jnp.pad(field, ((0, 0), (0, 0), (0, 0), (1, 1)))
    beside = beside + zpad[..., 2:] + zpad[..., :-2]
    return shift * field + stiff * (6.0 * field - beside)


def fine_apply(field, stiff, shift):
    padded = with_halo(field, (("gx", 1), ("gy", 2)), 1)
    return stencil(padded, field, stiff, shift)


def grid_apply(field, stiff, shift):
    padded = with_halo(field, (("gx", 1), ("gy", 2)), 1)
    return stencil(padded, field, stiff, shift)


def chebyshev(rhs, guess, steps, low, high, stiff, shift, from_zero, apply_op):
    theta = (high + low) / 2.0
    delta = (high - low) / 2.0
    sigma = theta / delta
    rho = 1.0 / sigma
    diagonal = shift + 6.0 * stiff
    resid = rhs if from_zero else rhs - apply_op(guess, stiff, shift)
    update = resid / (diagonal * theta)
    guess = guess + update
    for step in range(steps - 1):
        resid = rhs - apply_op(guess, stiff, shift)
        rho_next = 1.0 / (2.0 * sigma - rho)
        update = rho_next * rho * update + 2.0 * rho_next / delta * resid / diagonal
        guess = guess + update
        rho = rho_next
    return guess


def boxes(field):
    shape = field.shape
    lead = shape[:-3]
    grouped = field.reshape(lead + (shape[-3] // 2, 2, shape[-2] // 2, 2, shape[-1] // 2, 2))
    count = len(lead)
    return grouped.mean(axis=(count + 1, count + 3, count + 5))


def spread_up(field):
    return jnp.repeat(jnp.repeat(jnp.repeat(field, 2, axis=-3), 2, axis=-2), 2, axis=-1)


def local(load, modulus, anchor, wall_mask):
    blocks = jnp.repeat(jnp.repeat(jnp.repeat(wall_mask, 4, axis=0), 4, axis=1), 8, axis=2)
    stiff = modulus * (0.2 + blocks.astype(jnp.float32))
    zeros = jnp.zeros_like(load)
    pre = chebyshev(load, zeros, SMOOTH, 0.5, 2.0, stiff, anchor, True, fine_apply)
    fine_rest = load - fine_apply(pre, stiff, anchor)
    coarse_rest = boxes(fine_rest)
    coarse_stiff = boxes(stiff) / 4.0
    coarse_shift = boxes(anchor)
    coarse_fix = chebyshev(
        coarse_rest,
        jnp.zeros_like(coarse_rest),
        COARSE_STEPS,
        0.05,
        2.0,
        coarse_stiff,
        coarse_shift,
        True,
        grid_apply,
    )
    guess = pre + spread_up(coarse_fix)
    solution = chebyshev(load, guess, SMOOTH, 0.5, 2.0, stiff, anchor, False, fine_apply)
    remainder = load - fine_apply(solution, stiff, anchor)
    return (solution, remainder)


def solution(mesh):
    return jax.shard_map(
        local,
        mesh=mesh,
        in_specs=(
            P(None, "gx", "gy", None),
            P("gx", "gy", None),
            P("gx", "gy", None),
            P("gx", "gy", None),
        ),
        out_specs=(P(None, "gx", "gy", None), P(None, "gx", "gy", None)),
        check_vma=False,
    )
```

profile of v0, /device:TPU:121, one launch (start us, length us, event | category | flops | bytes accessed | tf_op | source)
XLA Modules:
  0.0 337.0 jit_solution(2583651560512096073)
XLA Ops:
  4.1 4.6 %collective-permute-start = (f32[3,1,16,128]{3,2,1,0:T(8,128)S(1)}, f32[3,1,16,128]{3,2,1,0:T(8,128)S(1)}, u32[]{:S(2)}, u32[]{:S(2)}) collective-permute-start(f32[3,1,16,128]{3,2,1,0:T(8,128)S(1)} %get-tuple-element.60), channel_id=1, source_target_pairs={{16,0},{32,16},{48,32},{64,48},{80,64},{96,80},{112,96},{128,112},... | collective-permute-start | bytes 73736 | tf_op jit(solution)/shard_map/ppermute | solution.py:20
  10.6 4.7 %collective-permute-done.1 = f32[3,1,16,128]{3,2,1,0:T(8,128)S(1)} collective-permute-done((f32[3,1,16,128]{3,2,1,0:T(8,128)S(1)}, f32[3,1,16,128]{3,2,1,0:T(8,128)S(1)}, u32[]{:S(2)}, u32[]{:S(2)}) %collective-permute-start.1) | collective-permute-done | bytes 24608 | tf_op jit(solution)/shard_map/ppermute | solution.py:18
  15.4 4.0 %collective-permute-start.2 = (f32[3,18,1,128]{3,2,1,0:T(1,128)S(1)}, f32[3,18,1,128]{3,2,1,0:T(1,128)S(1)}, u32[]{:S(2)}, u32[]{:S(2)}) collective-permute-start(f32[3,18,1,128]{3,2,1,0:T(1,128)S(1)} %get-tuple-element.45), channel_id=1, source_target_pairs={{1,0},{2,1},{3,2},{4,3},{5,4},{6,5},{7,6},{8,7},{9,8},{10,9},{11,1... | collective-permute-start | bytes 82952 | tf_op jit(solution)/shard_map/ppermute | solution.py:20
  19.4 4.7 %collective-permute-start.3 = (f32[3,18,1,128]{3,2,1,0:T(1,128)S(1)}, f32[3,18,1,128]{3,2,1,0:T(1,128)S(1)}, u32[]{:S(2)}, u32[]{:S(2)}) collective-permute-start(f32[3,18,1,128]{3,2,1,0:T(1,128)S(1)} %get-tuple-element.46), channel_id=1, source_target_pairs={{0,1},{1,2},{2,3},{3,4},{4,5},{5,6},{6,7},{7,8},{8,9},{9,10},{10,1... | collective-permute-start | bytes 82952 | tf_op jit(solution)/shard_map/ppermute | solution.py:18
  28.4 3.4 collective-permute-start.5
  31.8 3.8 %collective-permute-done.5 = f32[3,1,16,128]{3,2,1,0:T(8,128)S(1)} collective-permute-done((f32[3,1,16,128]{3,2,1,0:T(8,128)S(1)}, f32[3,1,16,128]{3,2,1,0:T(8,128)S(1)}, u32[]{:S(2)}, u32[]{:S(2)}) %collective-permute-start.5) | collective-permute-done | bytes 24608 | tf_op jit(solution)/shard_map/ppermute | solution.py:18
  38.0 5.6 %collective-permute-start.7 = (f32[3,18,1,128]{3,2,1,0:T(1,128)S(1)}, f32[3,18,1,128]{3,2,1,0:T(1,128)S(1)}, u32[]{:S(2)}, u32[]{:S(2)}) collective-permute-start(f32[3,18,1,128]{3,2,1,0:T(1,128)S(1)} %get-tuple-element.44), channel_id=1, source_target_pairs={{0,1},{1,2},{2,3},{3,4},{4,5},{5,6},{6,7},{7,8},{8,9},{9,10},{10,1... | collective-permute-start | bytes 82952 | tf_op jit(solution)/shard_map/ppermute | solution.py:18
  48.0 3.4 collective-permute-start.9
  51.4 9.8 %reshape.57 = f32[8,2,8,2,64,2]{5,4,3,2,1,0:T(8,128)} reshape(f32[16,16,128]{2,1,0:T(8,128)S(1)} %get-tuple-element.32) | data formatting | bytes 262144 | tf_op jit(solution)/shard_map/reshape | solution.py:66
  61.2 9.7 %reshape.56 = f32[8,2,8,2,64,2]{5,4,3,2,1,0:T(8,128)} reshape(f32[16,16,128]{2,1,0:T(8,128)S(1)} %copy-done.1) | data formatting | bytes 262144 | tf_op jit(solution)/shard_map/reshape | solution.py:66
  70.9 4.1 %reduce_sum.29 = f32[8,8,64]{2,1,0:T(8,128)S(1)} reduce(f32[8,2,8,2,64,2]{5,4,3,2,1,0:T(8,128)} %reshape.57, f32[]{:T(128)} %constant.9.clone.1), dimensions={1,3,5}, to_apply=%region_2.3 | reduce | flops 28672 | bytes 147460 | tf_op jit(solution)/shard_map/reduce_sum | solution.py:68
  75.0 4.0 %reduce_sum.28 = f32[8,8,64]{2,1,0:T(8,128)S(1)} reduce(f32[8,2,8,2,64,2]{5,4,3,2,1,0:T(8,128)} %reshape.56, f32[]{:T(128)} %constant.9.clone.1), dimensions={1,3,5}, to_apply=%region_1.2 | reduce | flops 28672 | bytes 147460 | tf_op jit(solution)/shard_map/reduce_sum | solution.py:68
  81.0 6.0 %collective-permute-start.11 = (f32[3,18,1,128]{3,2,1,0:T(1,128)S(1)}, f32[3,18,1,128]{3,2,1,0:T(1,128)S(1)}, u32[]{:S(2)}, u32[]{:S(2)}) collective-permute-start(f32[3,18,1,128]{3,2,1,0:T(1,128)S(1)} %get-tuple-element.42), channel_id=1, source_target_pairs={{0,1},{1,2},{2,3},{3,4},{4,5},{5,6},{6,7},{7,8},{8,9},{9,10},{10,1... | collective-permute-start | bytes 82952 | tf_op jit(solution)/shard_map/ppermute | solution.py:18
  88.3 26.6 %reshape.55 = f32[3,8,2,8,2,64,2]{6,5,4,3,2,1,0:T(8,128)} reshape(f32[3,16,16,128]{3,2,1,0:T(8,128)S(1)} %fusion.24) | data formatting | bytes 786432 | tf_op jit(solution)/shard_map/reshape | solution.py:66
  114.8 9.4 %reduce_sum.27 = f32[3,8,8,64]{3,2,1,0:T(8,128)S(1)} reduce(f32[3,8,2,8,2,64,2]{6,5,4,3,2,1,0:T(8,128)} %reshape.55, f32[]{:T(128)} %constant.9.clone.1), dimensions={2,4,6}, to_apply=%region_0.1 | reduce | flops 86016 | bytes 442372 | tf_op jit(solution)/shard_map/reduce_sum | solution.py:68
  124.3 3.8 %collective-permute-start.12 = (f32[3,1,8,64]{3,2,1,0:T(8,128)S(1)}, f32[3,1,8,64]{3,2,1,0:T(8,128)S(1)}, u32[]{:S(2)}, u32[]{:S(2)}) collective-permute-start(f32[3,1,8,64]{3,2,1,0:T(8,128)S(1)} %get-tuple-element.88), channel_id=1, source_target_pairs={{16,0},{32,16},{48,32},{64,48},{80,64},{96,80},{112,96},{128,112},... | collective-permute-start | bytes 18440 | tf_op jit(solution)/shard_map/ppermute | solution.py:20
  130.0 4.6 %collective-permute-done.13 = f32[3,1,8,64]{3,2,1,0:T(8,128)S(1)} collective-permute-done((f32[3,1,8,64]{3,2,1,0:T(8,128)S(1)}, f32[3,1,8,64]{3,2,1,0:T(8,128)S(1)}, u32[]{:S(2)}, u32[]{:S(2)}) %collective-permute-start.13) | collective-permute-done | bytes 6176 | tf_op jit(solution)/shard_map/ppermute | solution.py:18
  136.6 6.9 %collective-permute-start.15 = (f32[3,10,1,64]{3,2,1,0:T(1,128)S(1)}, f32[3,10,1,64]{3,2,1,0:T(1,128)S(1)}, u32[]{:S(2)}, u32[]{:S(2)}) collective-permute-start(f32[3,10,1,64]{3,2,1,0:T(1,128)S(1)} %get-tuple-element.74), channel_id=1, source_target_pairs={{0,1},{1,2},{2,3},{3,4},{4,5},{5,6},{6,7},{7,8},{8,9},{9,10},{10,1... | collective-permute-start | bytes 23048 | tf_op jit(solution)/shard_map/ppermute | solution.py:18
  146.4 3.4 collective-permute-start.17
  149.7 3.2 collective-permute-done.17
  154.9 6.6 %collective-permute-start.19 = (f32[3,10,1,64]{3,2,1,0:T(1,128)S(1)}, f32[3,10,1,64]{3,2,1,0:T(1,128)S(1)}, u32[]{:S(2)}, u32[]{:S(2)}) collective-permute-start(f32[3,10,1,64]{3,2,1,0:T(1,128)S(1)} %get-tuple-element.72), channel_id=1, source_target_pairs={{0,1},{1,2},{2,3},{3,4},{4,5},{5,6},{6,7},{7,8},{8,9},{9,10},{10,1... | collective-permute-start | bytes 23048 | tf_op jit(solution)/shard_map/ppermute | solution.py:18
  164.4 3.4 collective-permute-start.21
  167.7 3.2 collective-permute-done.21
  172.9 6.6 %collective-permute-start.23 = (f32[3,10,1,64]{3,2,1,0:T(1,128)S(1)}, f32[3,10,1,64]{3,2,1,0:T(1,128)S(1)}, u32[]{:S(2)}, u32[]{:S(2)}) collective-permute-start(f32[3,10,1,64]{3,2,1,0:T(1,128)S(1)} %get-tuple-element.70), channel_id=1, source_target_pairs={{0,1},{1,2},{2,3},{3,4},{4,5},{5,6},{6,7},{7,8},{8,9},{9,10},{10,1... | collective-permute-start | bytes 23048 | tf_op jit(solution)/shard_map/ppermute | solution.py:18
  182.3 3.4 collective-permute-start.25
  185.7 3.2 collective-permute-done.25
  190.9 6.6 %collective-permute-start.27 = (f32[3,10,1,64]{3,2,1,0:T(1,128)S(1)}, f32[3,10,1,64]{3,2,1,0:T(1,128)S(1)}, u32[]{:S(2)}, u32[]{:S(2)}) collective-permute-start(f32[3,10,1,64]{3,2,1,0:T(1,128)S(1)} %get-tuple-element.68), channel_id=1, source_target_pairs={{0,1},{1,2},{2,3},{3,4},{4,5},{5,6},{6,7},{7,8},{8,9},{9,10},{10,1... | collective-permute-start | bytes 23048 | tf_op jit(solution)/shard_map/ppermute | solution.py:18
  200.3 3.4 collective-permute-start.29
  203.7 3.2 collective-permute-done.29
  208.8 6.6 %collective-permute-start.31 = (f32[3,10,1,64]{3,2,1,0:T(1,128)S(1)}, f32[3,10,1,64]{3,2,1,0:T(1,128)S(1)}, u32[]{:S(2)}, u32[]{:S(2)}) collective-permute-start(f32[3,10,1,64]{3,2,1,0:T(1,128)S(1)} %get-tuple-element.66), channel_id=1, source_target_pairs={{0,1},{1,2},{2,3},{3,4},{4,5},{5,6},{6,7},{7,8},{8,9},{9,10},{10,1... | collective-permute-start | bytes 23048 | tf_op jit(solution)/shard_map/ppermute | solution.py:18
  218.3 3.4 collective-permute-start.33
  221.7 3.2 collective-permute-done.33
  226.8 6.6 %collective-permute-start.35 = (f32[3,10,1,64]{3,2,1,0:T(1,128)S(1)}, f32[3,10,1,64]{3,2,1,0:T(1,128)S(1)}, u32[]{:S(2)}, u32[]{:S(2)}) collective-permute-start(f32[3,10,1,64]{3,2,1,0:T(1,128)S(1)} %get-tuple-element.64), channel_id=1, source_target_pairs={{0,1},{1,2},{2,3},{3,4},{4,5},{5,6},{6,7},{7,8},{8,9},{9,10},{10,1... | collective-permute-start | bytes 23048 | tf_op jit(solution)/shard_map/ppermute | solution.py:18
  236.3 3.4 collective-permute-start.37
  239.7 3.2 collective-permute-done.37
  244.8 6.7 %collective-permute-start.39 = (f32[3,10,1,64]{3,2,1,0:T(1,128)S(1)}, f32[3,10,1,64]{3,2,1,0:T(1,128)S(1)}, u32[]{:S(2)}, u32[]{:S(2)}) collective-permute-start(f32[3,10,1,64]{3,2,1,0:T(1,128)S(1)} %get-tuple-element.62), channel_id=1, source_target_pairs={{0,1},{1,2},{2,3},{3,4},{4,5},{5,6},{6,7},{7,8},{8,9},{9,10},{10,1... | collective-permute-start | bytes 23048 | tf_op jit(solution)/shard_map/ppermute | solution.py:18
  260.9 3.4 collective-permute-start.41
  264.3 3.3 collective-permute-done.41
  269.6 6.6 %collective-permute-start.43 = (f32[3,18,1,128]{3,2,1,0:T(1,128)S(1)}, f32[3,18,1,128]{3,2,1,0:T(1,128)S(1)}, u32[]{:S(2)}, u32[]{:S(2)}) collective-permute-start(f32[3,18,1,128]{3,2,1,0:T(1,128)S(1)} %get-tuple-element.40), channel_id=1, source_target_pairs={{0,1},{1,2},{2,3},{3,4},{4,5},{5,6},{6,7},{7,8},{8,9},{9,10},{10,1... | collective-permute-start | bytes 82952 | tf_op jit(solution)/shard_map/ppermute | solution.py:18
  280.5 3.4 collective-permute-start.45
  283.8 3.3 collective-permute-done.45
  289.1 6.6 %collective-permute-start.47 = (f32[3,18,1,128]{3,2,1,0:T(1,128)S(1)}, f32[3,18,1,128]{3,2,1,0:T(1,128)S(1)}, u32[]{:S(2)}, u32[]{:S(2)}) collective-permute-start(f32[3,18,1,128]{3,2,1,0:T(1,128)S(1)} %get-tuple-element.38), channel_id=1, source_target_pairs={{0,1},{1,2},{2,3},{3,4},{4,5},{5,6},{6,7},{7,8},{8,9},{9,10},{10,1... | collective-permute-start | bytes 82952 | tf_op jit(solution)/shard_map/ppermute | solution.py:18
  300.1 3.4 collective-permute-start.49
  303.4 3.3 collective-permute-done.49
  308.7 6.6 %collective-permute-start.51 = (f32[3,18,1,128]{3,2,1,0:T(1,128)S(1)}, f32[3,18,1,128]{3,2,1,0:T(1,128)S(1)}, u32[]{:S(2)}, u32[]{:S(2)}) collective-permute-start(f32[3,18,1,128]{3,2,1,0:T(1,128)S(1)} %get-tuple-element.36), channel_id=1, source_target_pairs={{0,1},{1,2},{2,3},{3,4},{4,5},{5,6},{6,7},{7,8},{8,9},{9,10},{10,1... | collective-permute-start | bytes 82952 | tf_op jit(solution)/shard_map/ppermute | solution.py:18
  319.7 3.4 collective-permute-start.53
  323.1 3.3 collective-permute-done.53
  328.3 6.6 %collective-permute-start.55 = (f32[3,18,1,128]{3,2,1,0:T(1,128)S(1)}, f32[3,18,1,128]{3,2,1,0:T(1,128)S(1)}, u32[]{:S(2)}, u32[]{:S(2)}) collective-permute-start(f32[3,18,1,128]{3,2,1,0:T(1,128)S(1)} %get-tuple-element.34), channel_id=1, source_target_pairs={{0,1},{1,2},{2,3},{3,4},{4,5},{5,6},{6,7},{7,8},{8,9},{9,10},{10,1... | collective-permute-start | bytes 82952 | tf_op jit(solution)/shard_map/ppermute | solution.py:18
  (148 shorter events, 84.7 us)
Async XLA Ops:
  4.1 6.5 %collective-permute-start = (f32[3,1,16,128]{3,2,1,0:T(8,128)S(1)}, f32[3,1,16,128]{3,2,1,0:T(8,128)S(1)}, u32[]{:S(2)}, u32[]{:S(2)}) collective-permute-start(f32[3,1,16,128]{3,2,1,0:T(8,128)S(1)} %get-tuple-element.60), channel_id=1, source_target_pairs={{16,0},{32,16},{48,32},{64,48},{80,64},{96,80},{112,96},{128,112},... | collective-permute-start | bytes 73736 | tf_op jit(solution)/shard_map/ppermute | solution.py:20
  8.7 6.7 %collective-permute-start.1 = (f32[3,1,16,128]{3,2,1,0:T(8,128)S(1)}, f32[3,1,16,128]{3,2,1,0:T(8,128)S(1)}, u32[]{:S(2)}, u32[]{:S(2)}) collective-permute-start(f32[3,1,16,128]{3,2,1,0:T(8,128)S(1)} %get-tuple-element.59), channel_id=1, source_target_pairs={{0,16},{16,32},{32,48},{48,64},{64,80},{80,96},{96,112},{112,128},... | collective-permute-start | bytes 73736 | tf_op jit(solution)/shard_map/ppermute | solution.py:18
  15.4 8.7 %collective-permute-start.2 = (f32[3,18,1,128]{3,2,1,0:T(1,128)S(1)}, f32[3,18,1,128]{3,2,1,0:T(1,128)S(1)}, u32[]{:S(2)}, u32[]{:S(2)}) collective-permute-start(f32[3,18,1,128]{3,2,1,0:T(1,128)S(1)} %get-tuple-element.45), channel_id=1, source_target_pairs={{1,0},{2,1},{3,2},{4,3},{5,4},{6,5},{7,6},{8,7},{9,8},{10,9},{11,1... | collective-permute-start | bytes 82952 | tf_op jit(solution)/shard_map/ppermute | solution.py:20
  19.4 5.6 %collective-permute-start.3 = (f32[3,18,1,128]{3,2,1,0:T(1,128)S(1)}, f32[3,18,1,128]{3,2,1,0:T(1,128)S(1)}, u32[]{:S(2)}, u32[]{:S(2)}) collective-permute-start(f32[3,18,1,128]{3,2,1,0:T(1,128)S(1)} %get-tuple-element.46), channel_id=1, source_target_pairs={{0,1},{1,2},{2,3},{3,4},{4,5},{5,6},{6,7},{7,8},{8,9},{9,10},{10,1... | collective-permute-start | bytes 82952 | tf_op jit(solution)/shard_map/ppermute | solution.py:18
  26.5 5.3 %collective-permute-start.4 = (f32[3,1,16,128]{3,2,1,0:T(8,128)S(1)}, f32[3,1,16,128]{3,2,1,0:T(8,128)S(1)}, u32[]{:S(2)}, u32[]{:S(2)}) collective-permute-start(f32[3,1,16,128]{3,2,1,0:T(8,128)S(1)} %get-tuple-element.58), channel_id=1, source_target_pairs={{16,0},{32,16},{48,32},{64,48},{80,64},{96,80},{112,96},{128,112},... | collective-permute-start | bytes 73736 | tf_op jit(solution)/shard_map/ppermute | solution.py:20
  28.4 7.2 %collective-permute-start.5 = (f32[3,1,16,128]{3,2,1,0:T(8,128)S(1)}, f32[3,1,16,128]{3,2,1,0:T(8,128)S(1)}, u32[]{:S(2)}, u32[]{:S(2)}) collective-permute-start(f32[3,1,16,128]{3,2,1,0:T(8,128)S(1)} %get-tuple-element.57), channel_id=1, source_target_pairs={{0,16},{16,32},{32,48},{48,64},{64,80},{80,96},{96,112},{112,128},... | collective-permute-start | bytes 73736 | tf_op jit(solution)/shard_map/ppermute | solution.py:18
  35.7 8.0 %collective-permute-start.6 = (f32[3,18,1,128]{3,2,1,0:T(1,128)S(1)}, f32[3,18,1,128]{3,2,1,0:T(1,128)S(1)}, u32[]{:S(2)}, u32[]{:S(2)}) collective-permute-start(f32[3,18,1,128]{3,2,1,0:T(1,128)S(1)} %get-tuple-element.43), channel_id=1, source_target_pairs={{1,0},{2,1},{3,2},{4,3},{5,4},{6,5},{7,6},{8,7},{9,8},{10,9},{11,1... | collective-permute-start | bytes 82952 | tf_op jit(solution)/shard_map/ppermute | solution.py:20
  38.0 6.6 %collective-permute-start.7 = (f32[3,18,1,128]{3,2,1,0:T(1,128)S(1)}, f32[3,18,1,128]{3,2,1,0:T(1,128)S(1)}, u32[]{:S(2)}, u32[]{:S(2)}) collective-permute-start(f32[3,18,1,128]{3,2,1,0:T(1,128)S(1)} %get-tuple-element.44), channel_id=1, source_target_pairs={{0,1},{1,2},{2,3},{3,4},{4,5},{5,6},{6,7},{7,8},{8,9},{9,10},{10,1... | collective-permute-start | bytes 82952 | tf_op jit(solution)/shard_map/ppermute | solution.py:18
  46.1 32.9 %collective-permute-start.8 = (f32[3,1,16,128]{3,2,1,0:T(8,128)S(1)}, f32[3,1,16,128]{3,2,1,0:T(8,128)S(1)}, u32[]{:S(2)}, u32[]{:S(2)}) collective-permute-start(f32[3,1,16,128]{3,2,1,0:T(8,128)S(1)} %get-tuple-element.56), channel_id=1, source_target_pairs={{16,0},{32,16},{48,32},{64,48},{80,64},{96,80},{112,96},{128,112},... | collective-permute-start | bytes 73736 | tf_op jit(solution)/shard_map/ppermute | solution.py:20
  48.0 31.0 %collective-permute-start.9 = (f32[3,1,16,128]{3,2,1,0:T(8,128)S(1)}, f32[3,1,16,128]{3,2,1,0:T(8,128)S(1)}, u32[]{:S(2)}, u32[]{:S(2)}) collective-permute-start(f32[3,1,16,128]{3,2,1,0:T(8,128)S(1)} %get-tuple-element.55), channel_id=1, source_target_pairs={{0,16},{16,32},{32,48},{48,64},{64,80},{80,96},{96,112},{112,128},... | collective-permute-start | bytes 73736 | tf_op jit(solution)/shard_map/ppermute | solution.py:18
  79.0 7.9 %collective-permute-start.10 = (f32[3,18,1,128]{3,2,1,0:T(1,128)S(1)}, f32[3,18,1,128]{3,2,1,0:T(1,128)S(1)}, u32[]{:S(2)}, u32[]{:S(2)}) collective-permute-start(f32[3,18,1,128]{3,2,1,0:T(1,128)S(1)} %get-tuple-element.41), channel_id=1, source_target_pairs={{1,0},{2,1},{3,2},{4,3},{5,4},{6,5},{7,6},{8,7},{9,8},{10,9},{11,1... | collective-permute-start | bytes 82952 | tf_op jit(solution)/shard_map/ppermute | solution.py:20
  81.0 6.9 %collective-permute-start.11 = (f32[3,18,1,128]{3,2,1,0:T(1,128)S(1)}, f32[3,18,1,128]{3,2,1,0:T(1,128)S(1)}, u32[]{:S(2)}, u32[]{:S(2)}) collective-permute-start(f32[3,18,1,128]{3,2,1,0:T(1,128)S(1)} %get-tuple-element.42), channel_id=1, source_target_pairs={{0,1},{1,2},{2,3},{3,4},{4,5},{5,6},{6,7},{7,8},{8,9},{9,10},{10,1... | collective-permute-start | bytes 82952 | tf_op jit(solution)/shard_map/ppermute | solution.py:18
  124.3 5.7 %collective-permute-start.12 = (f32[3,1,8,64]{3,2,1,0:T(8,128)S(1)}, f32[3,1,8,64]{3,2,1,0:T(8,128)S(1)}, u32[]{:S(2)}, u32[]{:S(2)}) collective-permute-start(f32[3,1,8,64]{3,2,1,0:T(8,128)S(1)} %get-tuple-element.88), channel_id=1, source_target_pairs={{16,0},{32,16},{48,32},{64,48},{80,64},{96,80},{112,96},{128,112},... | collective-permute-start | bytes 18440 | tf_op jit(solution)/shard_map/ppermute | solution.py:20
  128.1 6.5 %collective-permute-start.13 = (f32[3,1,8,64]{3,2,1,0:T(8,128)S(1)}, f32[3,1,8,64]{3,2,1,0:T(8,128)S(1)}, u32[]{:S(2)}, u32[]{:S(2)}) collective-permute-start(f32[3,1,8,64]{3,2,1,0:T(8,128)S(1)} %get-tuple-element.87), channel_id=1, source_target_pairs={{0,16},{16,32},{32,48},{48,64},{64,80},{80,96},{96,112},{112,128},... | collective-permute-start | bytes 18440 | tf_op jit(solution)/shard_map/ppermute | solution.py:18
  134.6 8.8 %collective-permute-start.14 = (f32[3,10,1,64]{3,2,1,0:T(1,128)S(1)}, f32[3,10,1,64]{3,2,1,0:T(1,128)S(1)}, u32[]{:S(2)}, u32[]{:S(2)}) collective-permute-start(f32[3,10,1,64]{3,2,1,0:T(1,128)S(1)} %get-tuple-element.73), channel_id=1, source_target_pairs={{1,0},{2,1},{3,2},{4,3},{5,4},{6,5},{7,6},{8,7},{9,8},{10,9},{11,1... | collective-permute-start | bytes 23048 | tf_op jit(solution)/shard_map/ppermute | solution.py:20
  136.6 7.7 %collective-permute-start.15 = (f32[3,10,1,64]{3,2,1,0:T(1,128)S(1)}, f32[3,10,1,64]{3,2,1,0:T(1,128)S(1)}, u32[]{:S(2)}, u32[]{:S(2)}) collective-permute-start(f32[3,10,1,64]{3,2,1,0:T(1,128)S(1)} %get-tuple-element.74), channel_id=1, source_target_pairs={{0,1},{1,2},{2,3},{3,4},{4,5},{5,6},{6,7},{7,8},{8,9},{9,10},{10,1... | collective-permute-start | bytes 23048 | tf_op jit(solution)/shard_map/ppermute | solution.py:18
  146.4 6.5 %collective-permute-start.17 = (f32[3,1,8,64]{3,2,1,0:T(8,128)S(1)}, f32[3,1,8,64]{3,2,1,0:T(8,128)S(1)}, u32[]{:S(2)}, u32[]{:S(2)}) collective-permute-start(f32[3,1,8,64]{3,2,1,0:T(8,128)S(1)} %get-tuple-element.85), channel_id=1, source_target_pairs={{0,16},{16,32},{32,48},{48,64},{64,80},{80,96},{96,112},{112,128},... | collective-permute-start | bytes 18440 | tf_op jit(solution)/shard_map/ppermute | solution.py:18
  152.9 8.5 %collective-permute-start.18 = (f32[3,10,1,64]{3,2,1,0:T(1,128)S(1)}, f32[3,10,1,64]{3,2,1,0:T(1,128)S(1)}, u32[]{:S(2)}, u32[]{:S(2)}) collective-permute-start(f32[3,10,1,64]{3,2,1,0:T(1,128)S(1)} %get-tuple-element.71), channel_id=1, source_target_pairs={{1,0},{2,1},{3,2},{4,3},{5,4},{6,5},{7,6},{8,7},{9,8},{10,9},{11,1... | collective-permute-start | bytes 23048 | tf_op jit(solution)/shard_map/ppermute | solution.py:20
  154.9 7.4 %collective-permute-start.19 = (f32[3,10,1,64]{3,2,1,0:T(1,128)S(1)}, f32[3,10,1,64]{3,2,1,0:T(1,128)S(1)}, u32[]{:S(2)}, u32[]{:S(2)}) collective-permute-start(f32[3,10,1,64]{3,2,1,0:T(1,128)S(1)} %get-tuple-element.72), channel_id=1, source_target_pairs={{0,1},{1,2},{2,3},{3,4},{4,5},{5,6},{6,7},{7,8},{8,9},{9,10},{10,1... | collective-permute-start | bytes 23048 | tf_op jit(solution)/shard_map/ppermute | solution.py:18
  162.4 5.3 %collective-permute-start.20 = (f32[3,1,8,64]{3,2,1,0:T(8,128)S(1)}, f32[3,1,8,64]{3,2,1,0:T(8,128)S(1)}, u32[]{:S(2)}, u32[]{:S(2)}) collective-permute-start(f32[3,1,8,64]{3,2,1,0:T(8,128)S(1)} %get-tuple-element.84), channel_id=1, source_target_pairs={{16,0},{32,16},{48,32},{64,48},{80,64},{96,80},{112,96},{128,112},... | collective-permute-start | bytes 18440 | tf_op jit(solution)/shard_map/ppermute | solution.py:20
  164.4 6.5 %collective-permute-start.21 = (f32[3,1,8,64]{3,2,1,0:T(8,128)S(1)}, f32[3,1,8,64]{3,2,1,0:T(8,128)S(1)}, u32[]{:S(2)}, u32[]{:S(2)}) collective-permute-start(f32[3,1,8,64]{3,2,1,0:T(8,128)S(1)} %get-tuple-element.83), channel_id=1, source_target_pairs={{0,16},{16,32},{32,48},{48,64},{64,80},{80,96},{96,112},{112,128},... | collective-permute-start | bytes 18440 | tf_op jit(solution)/shard_map/ppermute | solution.py:18
  170.9 8.5 %collective-permute-start.22 = (f32[3,10,1,64]{3,2,1,0:T(1,128)S(1)}, f32[3,10,1,64]{3,2,1,0:T(1,128)S(1)}, u32[]{:S(2)}, u32[]{:S(2)}) collective-permute-start(f32[3,10,1,64]{3,2,1,0:T(1,128)S(1)} %get-tuple-element.69), channel_id=1, source_target_pairs={{1,0},{2,1},{3,2},{4,3},{5,4},{6,5},{7,6},{8,7},{9,8},{10,9},{11,1... | collective-permute-start | bytes 23048 | tf_op jit(solution)/shard_map/ppermute | solution.py:20
  172.9 7.4 %collective-permute-start.23 = (f32[3,10,1,64]{3,2,1,0:T(1,128)S(1)}, f32[3,10,1,64]{3,2,1,0:T(1,128)S(1)}, u32[]{:S(2)}, u32[]{:S(2)}) collective-permute-start(f32[3,10,1,64]{3,2,1,0:T(1,128)S(1)} %get-tuple-element.70), channel_id=1, source_target_pairs={{0,1},{1,2},{2,3},{3,4},{4,5},{5,6},{6,7},{7,8},{8,9},{9,10},{10,1... | collective-permute-start | bytes 23048 | tf_op jit(solution)/shard_map/ppermute | solution.py:18
  182.3 6.5 %collective-permute-start.25 = (f32[3,1,8,64]{3,2,1,0:T(8,128)S(1)}, f32[3,1,8,64]{3,2,1,0:T(8,128)S(1)}, u32[]{:S(2)}, u32[]{:S(2)}) collective-permute-start(f32[3,1,8,64]{3,2,1,0:T(8,128)S(1)} %get-tuple-element.81), channel_id=1, source_target_pairs={{0,16},{16,32},{32,48},{48,64},{64,80},{80,96},{96,112},{112,128},... | collective-permute-start | bytes 18440 | tf_op jit(solution)/shard_map/ppermute | solution.py:18
  188.9 8.5 %collective-permute-start.26 = (f32[3,10,1,64]{3,2,1,0:T(1,128)S(1)}, f32[3,10,1,64]{3,2,1,0:T(1,128)S(1)}, u32[]{:S(2)}, u32[]{:S(2)}) collective-permute-start(f32[3,10,1,64]{3,2,1,0:T(1,128)S(1)} %get-tuple-element.67), channel_id=1, source_target_pairs={{1,0},{2,1},{3,2},{4,3},{5,4},{6,5},{7,6},{8,7},{9,8},{10,9},{11,1... | collective-permute-start | bytes 23048 | tf_op jit(solution)/shard_map/ppermute | solution.py:20
  190.9 7.4 %collective-permute-start.27 = (f32[3,10,1,64]{3,2,1,0:T(1,128)S(1)}, f32[3,10,1,64]{3,2,1,0:T(1,128)S(1)}, u32[]{:S(2)}, u32[]{:S(2)}) collective-permute-start(f32[3,10,1,64]{3,2,1,0:T(1,128)S(1)} %get-tuple-element.68), channel_id=1, source_target_pairs={{0,1},{1,2},{2,3},{3,4},{4,5},{5,6},{6,7},{7,8},{8,9},{9,10},{10,1... | collective-permute-start | bytes 23048 | tf_op jit(solution)/shard_map/ppermute | solution.py:18
  198.4 5.3 %collective-permute-start.28 = (f32[3,1,8,64]{3,2,1,0:T(8,128)S(1)}, f32[3,1,8,64]{3,2,1,0:T(8,128)S(1)}, u32[]{:S(2)}, u32[]{:S(2)}) collective-permute-start(f32[3,1,8,64]{3,2,1,0:T(8,128)S(1)} %get-tuple-element.80), channel_id=1, source_target_pairs={{16,0},{32,16},{48,32},{64,48},{80,64},{96,80},{112,96},{128,112},... | collective-permute-start | bytes 18440 | tf_op jit(solution)/shard_map/ppermute | solution.py:20
  200.3 6.5 %collective-permute-start.29 = (f32[3,1,8,64]{3,2,1,0:T(8,128)S(1)}, f32[3,1,8,64]{3,2,1,0:T(8,128)S(1)}, u32[]{:S(2)}, u32[]{:S(2)}) collective-permute-start(f32[3,1,8,64]{3,2,1,0:T(8,128)S(1)} %get-tuple-element.79), channel_id=1, source_target_pairs={{0,16},{16,32},{32,48},{48,64},{64,80},{80,96},{96,112},{112,128},... | collective-permute-start | bytes 18440 | tf_op jit(solution)/shard_map/ppermute | solution.py:18
  206.9 8.5 %collective-permute-start.30 = (f32[3,10,1,64]{3,2,1,0:T(1,128)S(1)}, f32[3,10,1,64]{3,2,1,0:T(1,128)S(1)}, u32[]{:S(2)}, u32[]{:S(2)}) collective-permute-start(f32[3,10,1,64]{3,2,1,0:T(1,128)S(1)} %get-tuple-element.65), channel_id=1, source_target_pairs={{1,0},{2,1},{3,2},{4,3},{5,4},{6,5},{7,6},{8,7},{9,8},{10,9},{11,1... | collective-permute-start | bytes 23048 | tf_op jit(solution)/shard_map/ppermute | solution.py:20
  208.8 7.4 %collective-permute-start.31 = (f32[3,10,1,64]{3,2,1,0:T(1,128)S(1)}, f32[3,10,1,64]{3,2,1,0:T(1,128)S(1)}, u32[]{:S(2)}, u32[]{:S(2)}) collective-permute-start(f32[3,10,1,64]{3,2,1,0:T(1,128)S(1)} %get-tuple-element.66), channel_id=1, source_target_pairs={{0,1},{1,2},{2,3},{3,4},{4,5},{5,6},{6,7},{7,8},{8,9},{9,10},{10,1... | collective-permute-start | bytes 23048 | tf_op jit(solution)/shard_map/ppermute | solution.py:18
  218.3 6.5 %collective-permute-start.33 = (f32[3,1,8,64]{3,2,1,0:T(8,128)S(1)}, f32[3,1,8,64]{3,2,1,0:T(8,128)S(1)}, u32[]{:S(2)}, u32[]{:S(2)}) collective-permute-start(f32[3,1,8,64]{3,2,1,0:T(8,128)S(1)} %get-tuple-element.77), channel_id=1, source_target_pairs={{0,16},{16,32},{32,48},{48,64},{64,80},{80,96},{96,112},{112,128},... | collective-permute-start | bytes 18440 | tf_op jit(solution)/shard_map/ppermute | solution.py:18
  224.9 8.5 %collective-permute-start.34 = (f32[3,10,1,64]{3,2,1,0:T(1,128)S(1)}, f32[3,10,1,64]{3,2,1,0:T(1,128)S(1)}, u32[]{:S(2)}, u32[]{:S(2)}) collective-permute-start(f32[3,10,1,64]{3,2,1,0:T(1,128)S(1)} %get-tuple-element.63), channel_id=1, source_target_pairs={{1,0},{2,1},{3,2},{4,3},{5,4},{6,5},{7,6},{8,7},{9,8},{10,9},{11,1... | collective-permute-start | bytes 23048 | tf_op jit(solution)/shard_map/ppermute | solution.py:20
  226.8 7.4 %collective-permute-start.35 = (f32[3,10,1,64]{3,2,1,0:T(1,128)S(1)}, f32[3,10,1,64]{3,2,1,0:T(1,128)S(1)}, u32[]{:S(2)}, u32[]{:S(2)}) collective-permute-start(f32[3,10,1,64]{3,2,1,0:T(1,128)S(1)} %get-tuple-element.64), channel_id=1, source_target_pairs={{0,1},{1,2},{2,3},{3,4},{4,5},{5,6},{6,7},{7,8},{8,9},{9,10},{10,1... | collective-permute-start | bytes 23048 | tf_op jit(solution)/shard_map/ppermute | solution.py:18
  236.3 6.5 %collective-permute-start.37 = (f32[3,1,8,64]{3,2,1,0:T(8,128)S(1)}, f32[3,1,8,64]{3,2,1,0:T(8,128)S(1)}, u32[]{:S(2)}, u32[]{:S(2)}) collective-permute-start(f32[3,1,8,64]{3,2,1,0:T(8,128)S(1)} %get-tuple-element.75), channel_id=1, source_target_pairs={{0,16},{16,32},{32,48},{48,64},{64,80},{80,96},{96,112},{112,128},... | collective-permute-start | bytes 18440 | tf_op jit(solution)/shard_map/ppermute | solution.py:18
  242.9 8.7 %collective-permute-start.38 = (f32[3,10,1,64]{3,2,1,0:T(1,128)S(1)}, f32[3,10,1,64]{3,2,1,0:T(1,128)S(1)}, u32[]{:S(2)}, u32[]{:S(2)}) collective-permute-start(f32[3,10,1,64]{3,2,1,0:T(1,128)S(1)} %get-tuple-element.61), channel_id=1, source_target_pairs={{1,0},{2,1},{3,2},{4,3},{5,4},{6,5},{7,6},{8,7},{9,8},{10,9},{11,1... | collective-permute-start | bytes 23048 | tf_op jit(solution)/shard_map/ppermute | solution.py:20
  244.8 7.4 %collective-permute-start.39 = (f32[3,10,1,64]{3,2,1,0:T(1,128)S(1)}, f32[3,10,1,64]{3,2,1,0:T(1,128)S(1)}, u32[]{:S(2)}, u32[]{:S(2)}) collective-permute-start(f32[3,10,1,64]{3,2,1,0:T(1,128)S(1)} %get-tuple-element.62), channel_id=1, source_target_pairs={{0,1},{1,2},{2,3},{3,4},{4,5},{5,6},{6,7},{7,8},{8,9},{9,10},{10,1... | collective-permute-start | bytes 23048 | tf_op jit(solution)/shard_map/ppermute | solution.py:18
  260.9 6.7 %collective-permute-start.41 = (f32[3,1,16,128]{3,2,1,0:T(8,128)S(1)}, f32[3,1,16,128]{3,2,1,0:T(8,128)S(1)}, u32[]{:S(2)}, u32[]{:S(2)}) collective-permute-start(f32[3,1,16,128]{3,2,1,0:T(8,128)S(1)} %get-tuple-element.53), channel_id=1, source_target_pairs={{0,16},{16,32},{32,48},{48,64},{64,80},{80,96},{96,112},{112,128},... | collective-permute-start | bytes 73736 | tf_op jit(solution)/shard_map/ppermute | solution.py:18
  267.7 8.5 %collective-permute-start.42 = (f32[3,18,1,128]{3,2,1,0:T(1,128)S(1)}, f32[3,18,1,128]{3,2,1,0:T(1,128)S(1)}, u32[]{:S(2)}, u32[]{:S(2)}) collective-permute-start(f32[3,18,1,128]{3,2,1,0:T(1,128)S(1)} %get-tuple-element.39), channel_id=1, source_target_pairs={{1,0},{2,1},{3,2},{4,3},{5,4},{6,5},{7,6},{8,7},{9,8},{10,9},{11,1... | collective-permute-start | bytes 82952 | tf_op jit(solution)/shard_map/ppermute | solution.py:20
  269.6 7.5 %collective-permute-start.43 = (f32[3,18,1,128]{3,2,1,0:T(1,128)S(1)}, f32[3,18,1,128]{3,2,1,0:T(1,128)S(1)}, u32[]{:S(2)}, u32[]{:S(2)}) collective-permute-start(f32[3,18,1,128]{3,2,1,0:T(1,128)S(1)} %get-tuple-element.40), channel_id=1, source_target_pairs={{0,1},{1,2},{2,3},{3,4},{4,5},{5,6},{6,7},{7,8},{8,9},{9,10},{10,1... | collective-permute-start | bytes 82952 | tf_op jit(solution)/shard_map/ppermute | solution.py:18
  280.5 6.7 %collective-permute-start.45 = (f32[3,1,16,128]{3,2,1,0:T(8,128)S(1)}, f32[3,1,16,128]{3,2,1,0:T(8,128)S(1)}, u32[]{:S(2)}, u32[]{:S(2)}) collective-permute-start(f32[3,1,16,128]{3,2,1,0:T(8,128)S(1)} %get-tuple-element.51), channel_id=1, source_target_pairs={{0,16},{16,32},{32,48},{48,64},{64,80},{80,96},{96,112},{112,128},... | collective-permute-start | bytes 73736 | tf_op jit(solution)/shard_map/ppermute | solution.py:18
  287.2 8.5 %collective-permute-start.46 = (f32[3,18,1,128]{3,2,1,0:T(1,128)S(1)}, f32[3,18,1,128]{3,2,1,0:T(1,128)S(1)}, u32[]{:S(2)}, u32[]{:S(2)}) collective-permute-start(f32[3,18,1,128]{3,2,1,0:T(1,128)S(1)} %get-tuple-element.37), channel_id=1, source_target_pairs={{1,0},{2,1},{3,2},{4,3},{5,4},{6,5},{7,6},{8,7},{9,8},{10,9},{11,1... | collective-permute-start | bytes 82952 | tf_op jit(solution)/shard_map/ppermute | solution.py:20
  289.1 7.5 %collective-permute-start.47 = (f32[3,18,1,128]{3,2,1,0:T(1,128)S(1)}, f32[3,18,1,128]{3,2,1,0:T(1,128)S(1)}, u32[]{:S(2)}, u32[]{:S(2)}) collective-permute-start(f32[3,18,1,128]{3,2,1,0:T(1,128)S(1)} %get-tuple-element.38), channel_id=1, source_target_pairs={{0,1},{1,2},{2,3},{3,4},{4,5},{5,6},{6,7},{7,8},{8,9},{9,10},{10,1... | collective-permute-start | bytes 82952 | tf_op jit(solution)/shard_map/ppermute | solution.py:18
  300.1 6.7 %collective-permute-start.49 = (f32[3,1,16,128]{3,2,1,0:T(8,128)S(1)}, f32[3,1,16,128]{3,2,1,0:T(8,128)S(1)}, u32[]{:S(2)}, u32[]{:S(2)}) collective-permute-start(f32[3,1,16,128]{3,2,1,0:T(8,128)S(1)} %get-tuple-element.49), channel_id=1, source_target_pairs={{0,16},{16,32},{32,48},{48,64},{64,80},{80,96},{96,112},{112,128},... | collective-permute-start | bytes 73736 | tf_op jit(solution)/shard_map/ppermute | solution.py:18
  306.8 8.5 %collective-permute-start.50 = (f32[3,18,1,128]{3,2,1,0:T(1,128)S(1)}, f32[3,18,1,128]{3,2,1,0:T(1,128)S(1)}, u32[]{:S(2)}, u32[]{:S(2)}) collective-permute-start(f32[3,18,1,128]{3,2,1,0:T(1,128)S(1)} %get-tuple-element.35), channel_id=1, source_target_pairs={{1,0},{2,1},{3,2},{4,3},{5,4},{6,5},{7,6},{8,7},{9,8},{10,9},{11,1... | collective-permute-start | bytes 82952 | tf_op jit(solution)/shard_map/ppermute | solution.py:20
  308.7 7.5 %collective-permute-start.51 = (f32[3,18,1,128]{3,2,1,0:T(1,128)S(1)}, f32[3,18,1,128]{3,2,1,0:T(1,128)S(1)}, u32[]{:S(2)}, u32[]{:S(2)}) collective-permute-start(f32[3,18,1,128]{3,2,1,0:T(1,128)S(1)} %get-tuple-element.36), channel_id=1, source_target_pairs={{0,1},{1,2},{2,3},{3,4},{4,5},{5,6},{6,7},{7,8},{8,9},{9,10},{10,1... | collective-permute-start | bytes 82952 | tf_op jit(solution)/shard_map/ppermute | solution.py:18
  319.7 6.7 %collective-permute-start.53 = (f32[3,1,16,128]{3,2,1,0:T(8,128)S(1)}, f32[3,1,16,128]{3,2,1,0:T(8,128)S(1)}, u32[]{:S(2)}, u32[]{:S(2)}) collective-permute-start(f32[3,1,16,128]{3,2,1,0:T(8,128)S(1)} %get-tuple-element.47), channel_id=1, source_target_pairs={{0,16},{16,32},{32,48},{48,64},{64,80},{80,96},{96,112},{112,128},... | collective-permute-start | bytes 73736 | tf_op jit(solution)/shard_map/ppermute | solution.py:18
  326.4 8.5 %collective-permute-start.54 = (f32[3,18,1,128]{3,2,1,0:T(1,128)S(1)}, f32[3,18,1,128]{3,2,1,0:T(1,128)S(1)}, u32[]{:S(2)}, u32[]{:S(2)}) collective-permute-start(f32[3,18,1,128]{3,2,1,0:T(1,128)S(1)} %get-tuple-element.33), channel_id=1, source_target_pairs={{1,0},{2,1},{3,2},{4,3},{5,4},{6,5},{7,6},{8,7},{9,8},{10,9},{11,1... | collective-permute-start | bytes 82952 | tf_op jit(solution)/shard_map/ppermute | solution.py:20
  328.3 7.5 %collective-permute-start.55 = (f32[3,18,1,128]{3,2,1,0:T(1,128)S(1)}, f32[3,18,1,128]{3,2,1,0:T(1,128)S(1)}, u32[]{:S(2)}, u32[]{:S(2)}) collective-permute-start(f32[3,18,1,128]{3,2,1,0:T(1,128)S(1)} %get-tuple-element.34), channel_id=1, source_target_pairs={{0,1},{1,2},{2,3},{3,4},{4,5},{5,6},{6,7},{7,8},{8,9},{9,10},{10,1... | collective-permute-start | bytes 82952 | tf_op jit(solution)/shard_map/ppermute | solution.py:18
  (17 other events, 486.7 us)
where the time goes:
time: 339 us; the launch traced here: 337 us
  starting transfers between devices  194 us (57%)
  waiting for transfers between devices  57.7 us (17%)
  local copies, waits for them, and re-layouts  52 us (15%)
  other arithmetic  31.7 us (9%)
    ppermute x28, starting transfers between devices, with_halo(): lax.ppermute(tail, axis, [(i, (i + 1) % count) for i in range(ends)])  133 us
    ppermute x28, starting transfers between devices, with_halo(): lax.ppermute(head, axis, [((i + 1) % count, i) for i in range(ends)])  60.8 us
    ppermute x28, waiting for transfers between devices, with_halo(): lax.ppermute(tail, axis, [(i, (i + 1) % count) for i in range(ends)])  57.6 us
    reshape x3, local copies, waits for them, and re-layouts, boxes(): field.reshape(lead + (shape[-3] // 2, 2, shape[-2] // 2, 2, shape[-1] //...  46 us
    reduce_sum x3, other arithmetic, boxes(): return grouped.mean(axis=(count + 1, count + 3, count + 5))  17.5 us
    add x12, other arithmetic, chebyshev(): guess = guess + update  8.19 us
  transfers between devices with their start and end apart: 56, of which 27 were waited for; matrix products, arithmetic and copies ran while one was open for 8% of the time, Pallas kernels for 0%

commit v1 on v0

v1 whole, which is shorter than its diff:
```python
import functools
import jax
import jax.numpy as jnp
from jax import lax
from jax.experimental import pallas as pl
from jax.experimental.pallas import tpu as pltpu
from jax.sharding import PartitionSpec as P

SMOOTH = 3
COARSE_STEPS = 8
MESH = pl.DeviceIdType.MESH

NEAR = [(-1, 0), (1, 0), (0, -1), (0, 1), (-1, -1), (-1, 1), (1, -1), (1, 1)]
FAR = [(-2, 0), (2, 0), (0, -2), (0, 2)]
KNIGHT = [(s * a, t * b) for a, b in ((2, 1), (1, 2)) for s in (-1, 1) for t in (-1, 1)]
ALL = NEAR + FAR + KNIGHT


def rates(low, high, steps):
    theta, delta = (high + low) / 2.0, (high - low) / 2.0
    sigma = theta / delta
    rho = 1.0 / sigma
    out = []
    for _ in range(steps - 1):
        rho_next = 1.0 / (2.0 * sigma - rho)
        out.append((rho_next * rho, 2.0 * rho_next / delta))
        rho = rho_next
    return theta, out


def around(src, planes, rows, ends, fold):
    x, (r0, n) = planes, rows
    first, last = ends
    v = src[0:3, x, r0 : r0 + n, :]
    below = src[0:3, x - 1, r0 : r0 + n, :]
    above = pltpu.roll(v, 64, 2) if fold else src[0:3, x + 1, r0 : r0 + n, :]
    nb = jnp.where(first, 0.0, pltpu.roll(v, 1, 2)) + jnp.where(last, 0.0, pltpu.roll(v, 127, 2))
    nb = nb + (below + above)
    nb = nb + (src[0:3, x, r0 - 1 : r0 + n - 1, :] + src[0:3, x, r0 + 1 : r0 + n + 1, :])
    return v, nb


def sweep(dst, src, prev, rhs, stiff, coefs, planes, rows, ends, fold_at=None):
    cv, cn, cb, cp = coefs
    r0, n = rows
    for x in planes:
        v, nb = around(src, x, rows, ends, x == fold_at)
        out = cv * v + (cn * stiff(x, r0, n))[None] * nb
        if cb:
            out = out + cb * rhs[0:3, x, r0 : r0 + n, :]
        if prev is not None:
            out = out + cp * prev[0:3, x, r0 : r0 + n, :]
        dst[0:3, x, r0 : r0 + n, :] = out


def kernel(
    nx, ny, load, modulus, anchor, mask, out_sol, out_rem,
    f_load, f_mod, f_anc, BK, XA, XC, DG, RM, SY, RY, SC, RC, SPY, RPY, SPC, RPC,
    ZC, LC, ZR, LH, IDC, PB, PK, Q, CB, CK, CX, CY, RB, RK, R2, RY2, RN, RM2, ZF,
    in_sem, out_sem, s1, r1, sk, rk, s2, r2, sp, rp,
):
    ix, iy = lax.axis_index("gx"), lax.axis_index("gy")

    def there(d):
        conds = []
        if d[0] < 0:
            conds.append(ix >= -d[0])
        if d[0] > 0:
            conds.append(ix < nx - d[0])
        if d[1] < 0:
            conds.append(iy >= -d[1])
        if d[1] > 0:
            conds.append(iy < ny - d[1])
        return functools.reduce(jnp.logical_and, conds)

    def device(d):
        return (ix + d[0], iy + d[1])

    def opposite(d):
        return (-d[0], -d[1])

    barrier = pltpu.get_barrier_semaphore()
    for d in ALL:

        @pl.when(there(d))
        def _():
            pl.semaphore_signal(barrier, inc=1, device_id=device(d), device_id_type=MESH)

    fetch = [
        pltpu.make_async_copy(modulus, f_mod, in_sem.at[0]),
        pltpu.make_async_copy(anchor, f_anc, in_sem.at[1]),
        pltpu.make_async_copy(load, f_load, in_sem.at[2]),
    ]
    for copy in fetch:
        copy.start()

    def lo_hi(s):
        return 0 if s < 0 else 1

    def first_from(d):
        if d[1] == 0:
            return BK.at[:, 1:4, 8:24, :] if d[0] < 0 else BK.at[:, 20:23, 8:24, :]
        if d[0] == 0:
            return RY.at[lo_hi(d[1])]
        return RC.at[2 * lo_hi(d[0]) + lo_hi(d[1])]

    def first_to(d):
        if d[1] == 0:
            return BK.at[:, 4:7, 8:24, :] if d[0] < 0 else BK.at[:, 17:20, 8:24, :]
        if d[0] == 0:
            return SY.at[lo_hi(d[1])]
        return SC.at[2 * lo_hi(d[0]) + lo_hi(d[1])]

    def pre_from(d):
        if d[1] == 0:
            return XC.at[:, 0:3, 8:24, :] if d[0] < 0 else XC.at[:, 21:24, 8:24, :]
        if d[0] == 0:
            return RPY.at[lo_hi(d[1])]
        return RPC.at[2 * lo_hi(d[0]) + lo_hi(d[1])]

    def pre_to(d):
        if d[1] == 0:
            return XC.at[:, 5:8, 8:24, :] if d[0] < 0 else XC.at[:, 16:19, 8:24, :]
        if d[0] == 0:
            return SPY.at[lo_hi(d[1])]
        return SPC.at[2 * lo_hi(d[0]) + lo_hi(d[1])]

    def stiff_from(d):
        if d[0] == 0:
            return CK.at[10:14, 8:16, :] if d[1] < 0 else CK.at[10:14, 24:32, :]
        return RK.at[lo_hi(d[0]), d[1] + 1]

    def stiff_to(d):
        return PK

    def coarse_from(d):
        if abs(d[0]) < 2 and abs(d[1]) < 2:
            if d[0] == 0:
                return CB.at[:, 10:14, 8:16, :] if d[1] < 0 else CB.at[:, 10:14, 24:32, :]
            return RB.at[lo_hi(d[0]), d[1] + 1]
        if d[1] == 0:
            return R2.at[lo_hi(d[0])]
        if d[0] == 0:
            return RY2.at[lo_hi(d[1])]
        if abs(d[0]) == 2:
            return RN.at[lo_hi(d[0]), lo_hi(d[1])]
        return RM2.at[lo_hi(d[0]), lo_hi(d[1])]

    def coarse_to(d):
        if abs(d[0]) < 2 and abs(d[1]) < 2:
            return PB
        if d[1] == 0:
            return PB.at[:, 0]
        if d[0] == 0:
            return Q.at[lo_hi(d[1])]
        return Q.at[lo_hi(d[1]), 0]

    def exchange(partners, to, came, send, recv):
        def copy(k, d):
            return pltpu.make_async_remote_copy(
                src_ref=to(d), dst_ref=came(opposite(d)), send_sem=send.at[k], recv_sem=recv.at[k],
                device_id=device(d), device_id_type=MESH,
            )

        def start():
            for k, d in enumerate(partners):

                @pl.when(there(d))
                def _():
                    copy(k, d).start()

        def wait():
            for k, d in enumerate(partners):

                @pl.when(there(opposite(d)))
                def _():
                    copy(k, d).wait_recv()

        def drain():
            for k, d in enumerate(partners):

                @pl.when(there(d))
                def _():
                    copy(k, d).wait_send()

        return start, wait, drain

    one = exchange(NEAR, first_to, first_from, s1, r1)
    pre = exchange(NEAR, pre_to, pre_from, sp, rp)
    kay = exchange(NEAR, stiff_to, stiff_from, sk, rk)
    two = exchange(ALL, coarse_to, coarse_from, s2, r2)

    for partners, came in ((NEAR, first_from), (NEAR, pre_from), (NEAR, stiff_from), (ALL, coarse_from)):
        for d in partners:

            @pl.when(jnp.logical_not(there(d)))
            def _():
                place = came(d)
                place[...] = jnp.zeros(place.shape, jnp.float32)

    spread = (
        lax.broadcasted_iota(jnp.int32, (16, 128), 1) // 8 == lax.broadcasted_iota(jnp.int32, (16, 128), 0)
    ).astype(jnp.float32)
    rows4 = (
        lax.broadcasted_iota(jnp.int32, (16, 4), 0) // 4 == lax.broadcasted_iota(jnp.int32, (16, 4), 1)
    ).astype(jnp.float32)
    fetch[0].wait()
    fetch[1].wait()
    for b in range(4):
        wall = jnp.dot(mask[b].astype(jnp.float32), spread, preferred_element_type=jnp.float32)
        wall = jnp.dot(rows4, wall, preferred_element_type=jnp.float32)
        for x in range(4 * b, 4 * b + 4):
            stiff = f_mod[x] * (0.2 + wall)
            diag = f_anc[x] + 6.0 * stiff
            inv = 1.0 / diag
            DG[0, x] = diag
            DG[1, x] = inv
            BK[3, 4 + x, 8:24, :] = stiff * inv
            f_mod[x] = stiff
    fetch[2].wait()
    for x in range(16):
        BK[0:3, 4 + x, 8:24, :] = f_load[:, x] * DG[1, x][None]
    for x in range(16):
        SY[0, :, x] = BK[:, 4 + x, 8:12, :]
        SY[1, :, x] = BK[:, 4 + x, 20:24, :]
    for cx, x0 in ((0, 4), (1, 18)):
        SC[2 * cx] = BK[:, x0 : x0 + 2, 8:12, :]
        SC[2 * cx + 1] = BK[:, x0 : x0 + 2, 20:24, :]

    pl.semaphore_wait(barrier, sum(there(d).astype(jnp.int32) for d in ALL))
    one[0]()

    pair_sum = 0.125 * (
        lax.broadcasted_iota(jnp.int32, (256, 128), 0) // 2 == lax.broadcasted_iota(jnp.int32, (256, 128), 1)
    ).astype(jnp.float32)

    def gather_pairs(place, lhs, f):
        for c in range(8):
            v = place[f, c, pl.ds(0, 8, 2), :] + place[f, c, pl.ds(1, 8, 2), :]
            if c < 4:
                lhs[f, c, :, 0:128] = v
            else:
                lhs[f, 7 - c, :, 128:256] = v

    def boxes(lhs, count):
        flat = lhs[...].reshape(count * 32, 256)
        return jnp.dot(flat, pair_sum, precision=lax.Precision.HIGHEST, preferred_element_type=jnp.float32)

    for c in range(8):
        ZC[0, c] = f_mod[2 * c] + f_mod[2 * c + 1]
        ZC[1, c] = f_anc[2 * c] + f_anc[2 * c + 1]
    gather_pairs(ZC, LC, 0)
    gather_pairs(ZC, LC, 1)
    means = boxes(LC, 2)
    coarse_stiff = 0.25 * means[0:32]
    inv = 1.0 / (means[32:64] + 6.0 * coarse_stiff)
    IDC[...] = inv.reshape(4, 8, 128)
    coarse_k = (coarse_stiff * inv).reshape(4, 8, 128)
    PK[...] = coarse_k
    CK[10:14, 16:24, :] = coarse_k
    kay[0]()

    lane = lax.broadcasted_iota(jnp.int32, (3, 24, 128), 2)
    ends = (lane == 0, lane == 127)
    short = (ends[0][:, :16], ends[1][:, :16])
    theta, ((a1, b1), (a2, b2)) = rates(0.5, 2.0, SMOOTH)

    def fine_k(x, r0, n):
        return BK[3, x, r0 : r0 + n, :]

    one[1]()
    for x in range(16):
        BK[:, 4 + x, 4:8, :] = RY[0, :, x]
        BK[:, 4 + x, 24:28, :] = RY[1, :, x]
    for cx, x0 in ((0, 2), (1, 20)):
        BK[:, x0 : x0 + 2, 4:8, :] = RC[2 * cx]
        BK[:, x0 : x0 + 2, 24:28, :] = RC[2 * cx + 1]
    wide = (4, 24)
    sweep(XA, BK, None, BK, fine_k, ((1.0 + a1 - b1) / theta + b1, b1 / theta, 0.0, 0.0), range(2, 22), wide, ends)
    sweep(XC, XA, None, BK, fine_k, (1.0 + a2 - b2, b2, b2 - a2 / theta, 0.0), range(3, 21), wide, ends)

    for c in range(8):
        total = 0.0
        for x in (4 + 2 * c, 5 + 2 * c):
            v, nb = around(XC, x, (8, 16), short, False)
            total = total + DG[0, x - 4][None] * (BK[0:3, x, 8:24, :] - v + fine_k(x, 8, 16)[None] * nb)
        ZR[:, c] = total
    for f in range(3):
        gather_pairs(ZR, LH, f)
    rest = boxes(LH, 3).reshape(3, 4, 8, 128) * IDC[...][None]
    PB[...] = rest
    for j in range(4):
        Q[0, j, 0:3] = rest[:, j, 0, :]
        Q[1, j, 0:3] = rest[:, j, 7, :]
    two[0]()
    CB[:, 10:14, 16:24, :] = rest

    for x in range(16):
        SPY[0, :, x] = XC[:, 4 + x, 8:12, :]
        SPY[1, :, x] = XC[:, 4 + x, 20:24, :]
    for cx, x0 in ((0, 4), (1, 17)):
        SPC[2 * cx] = XC[:, x0 : x0 + 3, 8:12, :]
        SPC[2 * cx + 1] = XC[:, x0 : x0 + 3, 20:24, :]
    pre[0]()

    left = lax.broadcasted_iota(jnp.int32, (8, 128), 1) < 64

    def meet(lo, hi):
        return pltpu.roll(jnp.where(left[: lo.shape[-2]], hi, lo), 64, lo.ndim - 1)

    kay[1]()
    for y in range(3):
        rows = slice(8 + 8 * y, 16 + 8 * y)
        for j in range(4):
            lo, hi = RK[0, y, j], RK[1, y, j]
            CK[2 + j, rows, :] = jnp.where(left, lo, hi)
            CK[9 - j, rows, :] = meet(lo, hi)
    two[1]()
    for y in range(3):
        rows = slice(8 + 8 * y, 16 + 8 * y)
        for j in range(4):
            for f in range(3):
                lo, hi = RB[0, y, f, j], RB[1, y, f, j]
                CB[f, 2 + j, rows, :] = jnp.where(left, lo, hi)
                CB[f, 9 - j, rows, :] = meet(lo, hi)
    for f in range(3):
        CB[f, 1, 16:24, :] = meet(R2[0, f], R2[1, f])
    for y, near, far in ((0, 15, 7), (1, 24, 32)):
        near_row = meet(RN[0, y, 0:3], RN[1, y, 0:3])
        far_row = meet(RM2[0, y, 0:3], RM2[1, y, 0:3])
        for f in range(3):
            CB[f, 1, near : near + 1, :] = near_row[f : f + 1]
            CB[f, 9, far : far + 1, :] = far_row[f : f + 1]
            for j in range(4):
                CB[f, 10 + j, far : far + 1, :] = RY2[y, j, f : f + 1]

    lane = lane % 64
    ends_c = (lane == 0, lane == 63)
    short_c = (ends_c[0][:, :16], ends_c[1][:, :16])
    theta_c, steps = rates(0.05, 2.0, COARSE_STEPS)

    def coarse_k_at(x, r0, n):
        return CK[x, r0 : r0 + n, :]

    at = CB
    for t in range(2, COARSE_STEPS + 1):
        a, b = steps[t - 2]
        rows, e = ((8, 24), ends_c) if t < 6 else ((12, 16), short_c)
        to = CY if t % 2 == 0 else CX
        if t == 2:
            coefs, prev = ((1.0 + a - b) / theta_c + b, b / theta_c, 0.0, 0.0), None
        elif t == 3:
            coefs, prev = (1.0 + a - b, b, b - a / theta_c, 0.0), None
        else:
            coefs, prev = (1.0 + a - b, b, b, -a), to
        sweep(to, at, prev, CB, coarse_k_at, coefs, range(t, 14), rows, e, 13)
        at = to

    repeat = (
        lax.broadcasted_iota(jnp.int32, (128, 256), 1) // 2 == lax.broadcasted_iota(jnp.int32, (128, 256), 0)
    ).astype(jnp.float32)
    pre[1]()
    pre[2]()
    for x in range(16):
        XC[:, 4 + x, 4:8, :] = RPY[0, :, x]
        XC[:, 4 + x, 24:28, :] = RPY[1, :, x]
    for cx, x0 in ((0, 1), (1, 20)):
        XC[:, x0 : x0 + 3, 4:8, :] = RPC[2 * cx]
        XC[:, x0 : x0 + 3, 24:28, :] = RPC[2 * cx + 1]
    for f in range(3):
        for i in range(6):
            v = at[f, 8 + i, 14:26, :]
            ZF[f, i, pl.ds(0, 12, 2), :] = v
            ZF[f, i, pl.ds(1, 12, 2), :] = v
        up = jnp.dot(
            ZF[f].reshape(144, 128), repeat, precision=lax.Precision.HIGHEST, preferred_element_type=jnp.float32
        ).reshape(6, 24, 256)
        for i in range(6):
            for x, v in ((2 * i, up[i, :, 0:128]), (22 - 2 * i, up[i, :, 128:256])):
                XC[f, x, 4:28, :] = XC[f, x, 4:28, :] + v
                XC[f, x + 1, 4:28, :] = XC[f, x + 1, 4:28, :] + v

    sweep(XA, XC, None, BK, fine_k, (1.0 - 1.0 / theta, 1.0 / theta, 1.0 / theta, 0.0), range(1, 23), wide, ends)
    sweep(XC, XA, XC, BK, fine_k, (1.0 + a1 - b1, b1, b1, -a1), range(2, 22), wide, ends)
    sweep(XA, XC, XA, BK, fine_k, (1.0 + a2 - b2, b2, b2, -a2), range(3, 21), wide, ends)
    put = [
        pltpu.make_async_copy(XA.at[:, 4:20, 8:24, :], out_sol, out_sem.at[0]),
        pltpu.make_async_copy(RM, out_rem, out_sem.at[1]),
    ]
    put[0].start()
    for x in range(4, 20):
        v, nb = around(XA, x, (8, 16), short, False)
        RM[:, x - 4] = DG[0, x - 4][None] * (BK[0:3, x, 8:24, :] - v + fine_k(x, 8, 16)[None] * nb)
    put[1].start()
    for _, _, drain in (one, kay, two):
        drain()
    put[0].wait()
    put[1].wait()


def local(nx, ny, load, modulus, anchor, wall_mask):
    f32 = jnp.float32

    def vmem(*shape):
        return pltpu.VMEM(shape, f32)

    dma = pltpu.SemaphoreType.DMA
    anywhere = pl.BlockSpec(memory_space=pl.ANY)
    shape = jax.ShapeDtypeStruct((3, 16, 16, 128), f32)
    return pl.pallas_call(
        functools.partial(kernel, nx, ny),
        out_shape=(shape, shape),
        in_specs=[anywhere, anywhere, anywhere, pl.BlockSpec(memory_space=pltpu.VMEM)],
        out_specs=(anywhere, anywhere),
        scratch_shapes=[
            vmem(3, 16, 16, 128), vmem(16, 16, 128), vmem(16, 16, 128),
            vmem(4, 24, 32, 128), vmem(3, 24, 32, 128), vmem(3, 24, 32, 128),
            vmem(2, 16, 16, 128), vmem(3, 16, 16, 128),
            vmem(2, 4, 16, 4, 128), vmem(2, 4, 16, 4, 128), vmem(4, 4, 2, 4, 128), vmem(4, 4, 2, 4, 128),
            vmem(2, 3, 16, 4, 128), vmem(2, 3, 16, 4, 128), vmem(4, 3, 3, 4, 128), vmem(4, 3, 3, 4, 128),
            vmem(2, 8, 16, 128), vmem(2, 4, 8, 256), vmem(3, 8, 16, 128), vmem(3, 4, 8, 256),
            vmem(4, 8, 128), vmem(3, 4, 8, 128), vmem(4, 8, 128), vmem(2, 4, 4, 128),
            vmem(3, 14, 40, 128), vmem(14, 40, 128), vmem(3, 14, 40, 128), vmem(3, 14, 40, 128),
            vmem(2, 3, 3, 4, 8, 128), vmem(2, 3, 4, 8, 128), vmem(2, 3, 8, 128),
            vmem(2, 4, 4, 128), vmem(2, 2, 4, 128), vmem(2, 2, 4, 128),
            vmem(3, 6, 24, 128),
            dma((3,)), dma((2,)), dma((8,)), dma((8,)), dma((8,)), dma((8,)), dma((20,)), dma((20,)), dma((8,)), dma((8,)),
        ],
        compiler_params=pltpu.CompilerParams(collective_id=0, has_side_effects=True, vmem_limit_bytes=48 << 20),
    )(load, modulus, anchor, wall_mask)


def solution(mesh):
    return jax.shard_map(
        functools.partial(local, mesh.shape["gx"], mesh.shape["gy"]),
        mesh=mesh,
        in_specs=(
            P(None, "gx", "gy", None),
            P("gx", "gy", None),
            P("gx", "gy", None),
            P("gx", "gy", None),
        ),
        out_specs=(P(None, "gx", "gy", None), P(None, "gx", "gy", None)),
        check_vma=False,
    )
```

time: 339 us -> 31.6 us (0.09)
  starting transfers between devices: 194 us -> 0 us
  waiting for transfers between devices: 57.7 us -> 0 us
  local copies, waits for them, and re-layouts: 52 us -> 4.99 us
  other arithmetic: 31.7 us -> 0 us
  Pallas kernels: 0 us -> 25.8 us
    ppermute x56 -> x0, starting transfers between devices: 194 us -> none  [the longest x28 133 us: with_halo(): lax.ppermute(tail, axis, [(i, (i + 1) % count) for i in range(ends)])]
    ppermute x56 -> x0, waiting for transfers between devices: 57.7 us -> none  [the longest x28 57.6 us: with_halo(): lax.ppermute(tail, axis, [(i, (i + 1) % count) for i in range(ends)])]
    reshape x5 -> x0, local copies, waits for them, and re-layouts: 49.6 us -> none  [the longest x3 46 us: boxes(): field.reshape(lead + (shape[-3] // 2, 2, shape[-2] // 2, 2, shape[-1] //...]
    pallas_call x0 -> x1, Pallas kernels: none -> 25.8 us  [local(): pl.pallas_call(functools.partial(kernel, nx, ny), out_shape=(shape, shape...]
    reduce_sum x3 -> x0, other arithmetic: 17.5 us -> none  [boxes(): return grouped.mean(axis=(count + 1, count + 3, count + 5))]
    add x14 -> x0, other arithmetic: 10.1 us -> none  [the longest x12 8.19 us: chebyshev(): guess = guess + update]
    unnamed x18 -> x10, local copies, waits for them, and re-layouts: 0.04 us -> 4.99 us
  transfers between devices with their start and end apart: 56 -> 0, of which waited for: 27 -> 0; matrix products, arithmetic and copies ran while one was open for 8% -> 0% of each run, Pallas kernels for 0% -> 0%
where the time goes in v1:
time: 31.6 us; the launch traced here: 31.4 us
  Pallas kernels  25.8 us (82%)
  local copies, waits for them, and re-layouts  4.99 us (16%)
  between operations  0.65 us (2%)
    pallas_call x1, Pallas kernels, local(): pl.pallas_call(functools.partial(kernel, nx, ny), out_shape=(shape, shape...  25.8 us
    unnamed x10, local copies, waits for them, and re-layouts  4.99 us

profile of v1, /device:TPU:121, one launch (start us, length us, event | category | flops | bytes accessed | tf_op | source)
XLA Modules:
  0.0 31.4 jit_solution(13046823191619887317)
XLA Ops:
  0.6 0.0 copy-start
  0.6 1.0 %copy-done = f32[3,16,16,128]{3,2,1,0:T(8,128)S(1)} copy-done((f32[3,16,16,128]{3,2,1,0:T(8,128)S(1)}, f32[3,16,16,128]{3,2,1,0:T(8,128)}, u32[]{:S(2)}) %copy-start) | copy-done | bytes 393240
  1.6 0.0 copy-start.1
  1.6 0.9 %copy-done.1 = f32[16,16,128]{2,1,0:T(8,128)S(1)} copy-done((f32[16,16,128]{2,1,0:T(8,128)S(1)}, f32[16,16,128]{2,1,0:T(8,128)}, u32[]{:S(2)}) %copy-start.1) | copy-done | bytes 131096
  2.5 0.0 copy-start.2
  2.5 0.9 %copy-done.2 = f32[16,16,128]{2,1,0:T(8,128)S(1)} copy-done((f32[16,16,128]{2,1,0:T(8,128)S(1)}, f32[16,16,128]{2,1,0:T(8,128)}, u32[]{:S(2)}) %copy-start.2) | copy-done | bytes 131096
  3.4 0.0 copy-start.3
  3.4 0.7 %copy-done.3 = s32[4,4,16]{2,1,0:T(4,128)S(1)} copy-done((s32[4,4,16]{2,1,0:T(4,128)S(1)}, s32[4,4,16]{2,1,0:T(4,128)}, u32[]{:S(2)}) %copy-start.3) | copy-done | bytes 1048
  4.1 25.8 %shard_map.59 = (f32[3,16,16,128]{3,2,1,0:T(8,128)S(1)}, f32[3,16,16,128]{3,2,1,0:T(8,128)S(1)}) custom-call(f32[3,16,16,128]{3,2,1,0:T(8,128)S(1)} %copy-done, f32[16,16,128]{2,1,0:T(8,128)S(1)} %copy-done.1, f32[16,16,128]{2,1,0:T(8,128)S(1)} %copy-done.2, s32[4,4,16]{2,1,0:T(4,128)S(1)} %copy-done.3), custom_call_target="tpu_custom_call" | custom-call | tf_op jit(solution)/shard_map/pallas_call | solution.py:410
  29.9 0.7 %copy.8 = f32[3,16,16,128]{3,2,1,0:T(8,128)} copy(f32[3,16,16,128]{3,2,1,0:T(8,128)S(1)} %get-tuple-element.4) | data formatting | bytes 786432
  30.7 0.7 %copy.9 = f32[3,16,16,128]{3,2,1,0:T(8,128)} copy(f32[3,16,16,128]{3,2,1,0:T(8,128)S(1)} %get-tuple-element.5) | data formatting | bytes 786432
Async XLA Ops:
  0.6 1.0 %copy-start = (f32[3,16,16,128]{3,2,1,0:T(8,128)S(1)}, f32[3,16,16,128]{3,2,1,0:T(8,128)}, u32[]{:S(2)}) copy-start(f32[3,16,16,128]{3,2,1,0:T(8,128)} %load.1) | copy-start | bytes 1179652
  1.6 0.9 %copy-start.1 = (f32[16,16,128]{2,1,0:T(8,128)S(1)}, f32[16,16,128]{2,1,0:T(8,128)}, u32[]{:S(2)}) copy-start(f32[16,16,128]{2,1,0:T(8,128)} %modulus.1) | copy-start | bytes 393220
  2.5 0.9 %copy-start.2 = (f32[16,16,128]{2,1,0:T(8,128)S(1)}, f32[16,16,128]{2,1,0:T(8,128)}, u32[]{:S(2)}) copy-start(f32[16,16,128]{2,1,0:T(8,128)} %anchor.1) | copy-start | bytes 393220
  3.4 0.7 %copy-start.3 = (s32[4,4,16]{2,1,0:T(4,128)S(1)}, s32[4,4,16]{2,1,0:T(4,128)}, u32[]{:S(2)}) copy-start(s32[4,4,16]{2,1,0:T(4,128)} %mask.1) | copy-start | bytes 3076

commit v2 on v1

--- a/solution.py
+++ b/solution.py
@@ -54,10 +54,10 @@
 
 
 def kernel(
-    nx, ny, load, modulus, anchor, mask, out_sol, out_rem,
-    f_load, f_mod, f_anc, BK, XA, XC, DG, RM, SY, RY, SC, RC, SPY, RPY, SPC, RPC,
+    nx, ny, load, modulus, anchor, wall_mask, XC, BK, DG,
+    f_load, f_mod, f_anc, mask, INV, XA, SY, RY, SC, RC, SPY, RPY, SPC, RPC,
     ZC, LC, ZR, LH, IDC, PB, PK, Q, CB, CK, CX, CY, RB, RK, R2, RY2, RN, RM2, ZF,
-    in_sem, out_sem, s1, r1, sk, rk, s2, r2, sp, rp,
+    in_sem, s1, r1, sk, rk, s2, r2, sp, rp,
 ):
     ix, iy = lax.axis_index("gx"), lax.axis_index("gy")
 
@@ -89,7 +89,8 @@
     fetch = [
         pltpu.make_async_copy(modulus, f_mod, in_sem.at[0]),
         pltpu.make_async_copy(anchor, f_anc, in_sem.at[1]),
-        pltpu.make_async_copy(load, f_load, in_sem.at[2]),
+        pltpu.make_async_copy(wall_mask, mask, in_sem.at[2]),
+        pltpu.make_async_copy(load, f_load, in_sem.at[3]),
     ]
     for copy in fetch:
         copy.start()
@@ -206,6 +207,7 @@
     ).astype(jnp.float32)
     fetch[0].wait()
     fetch[1].wait()
+    fetch[2].wait()
     for b in range(4):
         wall = jnp.dot(mask[b].astype(jnp.float32), spread, preferred_element_type=jnp.float32)
         wall = jnp.dot(rows4, wall, preferred_element_type=jnp.float32)
@@ -213,13 +215,13 @@
             stiff = f_mod[x] * (0.2 + wall)
             diag = f_anc[x] + 6.0 * stiff
             inv = 1.0 / diag
-            DG[0, x] = diag
-            DG[1, x] = inv
+            DG[x] = diag
+            INV[x] = inv
             BK[3, 4 + x, 8:24, :] = stiff * inv
             f_mod[x] = stiff
-    fetch[2].wait()
+    fetch[3].wait()
     for x in range(16):
-        BK[0:3, 4 + x, 8:24, :] = f_load[:, x] * DG[1, x][None]
+        BK[0:3, 4 + x, 8:24, :] = f_load[:, x] * INV[x][None]
     for x in range(16):
         SY[0, :, x] = BK[:, 4 + x, 8:12, :]
         SY[1, :, x] = BK[:, 4 + x, 20:24, :]
@@ -283,7 +285,7 @@
         total = 0.0
         for x in (4 + 2 * c, 5 + 2 * c):
             v, nb = around(XC, x, (8, 16), short, False)
-            total = total + DG[0, x - 4][None] * (BK[0:3, x, 8:24, :] - v + fine_k(x, 8, 16)[None] * nb)
+            total = total + DG[x - 4][None] * (BK[0:3, x, 8:24, :] - v + fine_k(x, 8, 16)[None] * nb)
         ZR[:, c] = total
     for f in range(3):
         gather_pairs(ZR, LH, f)
@@ -379,10 +381,23 @@
             for x, v in ((2 * i, up[i, :, 0:128]), (22 - 2 * i, up[i, :, 128:256])):
                 XC[f, x, 4:28, :] = XC[f, x, 4:28, :] + v
                 XC[f, x + 1, 4:28, :] = XC[f, x + 1, 4:28, :] + v
+    for _, _, drain in (one, kay, two):
+        drain()
+
+
+def after(XC, BK, DG, out_sol, out_rem, XA, XB, RM, out_sem):
+    lane = lax.broadcasted_iota(jnp.int32, (3, 24, 128), 2)
+    ends = (lane == 0, lane == 127)
+    short = (ends[0][:, :16], ends[1][:, :16])
+    theta, ((a1, b1), (a2, b2)) = rates(0.5, 2.0, SMOOTH)
+    wide = (4, 24)
+
+    def fine_k(x, r0, n):
+        return BK[3, x, r0 : r0 + n, :]
 
     sweep(XA, XC, None, BK, fine_k, (1.0 - 1.0 / theta, 1.0 / theta, 1.0 / theta, 0.0), range(1, 23), wide, ends)
-    sweep(XC, XA, XC, BK, fine_k, (1.0 + a1 - b1, b1, b1, -a1), range(2, 22), wide, ends)
-    sweep(XA, XC, XA, BK, fine_k, (1.0 + a2 - b2, b2, b2, -a2), range(3, 21), wide, ends)
+    sweep(XB, XA, XC, BK, fine_k, (1.0 + a1 - b1, b1, b1, -a1), range(2, 22), wide, ends)
+    sweep(XA, XB, XA, BK, fine_k, (1.0 + a2 - b2, b2, b2, -a2), range(3, 21), wide, ends)
     put = [
         pltpu.make_async_copy(XA.at[:, 4:20, 8:24, :], out_sol, out_sem.at[0]),
         pltpu.make_async_copy(RM, out_rem, out_sem.at[1]),
@@ -390,10 +405,8 @@
     put[0].start()
     for x in range(4, 20):
         v, nb = around(XA, x, (8, 16), short, False)
-        RM[:, x - 4] = DG[0, x - 4][None] * (BK[0:3, x, 8:24, :] - v + fine_k(x, 8, 16)[None] * nb)
+        RM[:, x - 4] = DG[x - 4][None] * (BK[0:3, x, 8:24, :] - v + fine_k(x, 8, 16)[None] * nb)
     put[1].start()
-    for _, _, drain in (one, kay, two):
-        drain()
     put[0].wait()
     put[1].wait()
 
@@ -405,17 +418,20 @@
         return pltpu.VMEM(shape, f32)
 
     dma = pltpu.SemaphoreType.DMA
-    anywhere = pl.BlockSpec(memory_space=pl.ANY)
-    shape = jax.ShapeDtypeStruct((3, 16, 16, 128), f32)
-    return pl.pallas_call(
+    far = pl.BlockSpec(memory_space=pltpu.HBM)
+    near = pl.BlockSpec(memory_space=pltpu.VMEM)
+    inner = pl.pallas_call(
         functools.partial(kernel, nx, ny),
-        out_shape=(shape, shape),
-        in_specs=[anywhere, anywhere, anywhere, pl.BlockSpec(memory_space=pltpu.VMEM)],
-        out_specs=(anywhere, anywhere),
+        out_shape=(
+            jax.ShapeDtypeStruct((3, 24, 32, 128), f32),
+            jax.ShapeDtypeStruct((4, 24, 32, 128), f32),
+            jax.ShapeDtypeStruct((16, 16, 128), f32),
+        ),
+        in_specs=[far] * 4,
+        out_specs=(near, near, near),
         scratch_shapes=[
             vmem(3, 16, 16, 128), vmem(16, 16, 128), vmem(16, 16, 128),
-            vmem(4, 24, 32, 128), vmem(3, 24, 32, 128), vmem(3, 24, 32, 128),
-            vmem(2, 16, 16, 128), vmem(3, 16, 16, 128),
+            pltpu.VMEM((4, 4, 16), jnp.int32), vmem(16, 16, 128), vmem(3, 24, 32, 128),
             vmem(2, 4, 16, 4, 128), vmem(2, 4, 16, 4, 128), vmem(4, 4, 2, 4, 128), vmem(4, 4, 2, 4, 128),
             vmem(2, 3, 16, 4, 128), vmem(2, 3, 16, 4, 128), vmem(4, 3, 3, 4, 128), vmem(4, 3, 3, 4, 128),
             vmem(2, 8, 16, 128), vmem(2, 4, 8, 256), vmem(3, 8, 16, 128), vmem(3, 4, 8, 256),
@@ -424,10 +440,19 @@
             vmem(2, 3, 3, 4, 8, 128), vmem(2, 3, 4, 8, 128), vmem(2, 3, 8, 128),
             vmem(2, 4, 4, 128), vmem(2, 2, 4, 128), vmem(2, 2, 4, 128),
             vmem(3, 6, 24, 128),
-            dma((3,)), dma((2,)), dma((8,)), dma((8,)), dma((8,)), dma((8,)), dma((20,)), dma((20,)), dma((8,)), dma((8,)),
+            dma((4,)), dma((8,)), dma((8,)), dma((8,)), dma((8,)), dma((20,)), dma((20,)), dma((8,)), dma((8,)),
         ],
-        compiler_params=pltpu.CompilerParams(collective_id=0, has_side_effects=True, vmem_limit_bytes=48 << 20),
-    )(load, modulus, anchor, wall_mask)
+        compiler_params=pltpu.CompilerParams(collective_id=0, has_side_effects=True, vmem_limit_bytes=24 << 20),
+    )(*(pltpu.with_memory_space_constraint(a, pltpu.HBM) for a in (load, modulus, anchor, wall_mask)))
+    shape = jax.ShapeDtypeStruct((3, 16, 16, 128), f32)
+    return pl.pallas_call(
+        after,
+        out_shape=(shape, shape),
+        in_specs=[near] * 3,
+        out_specs=(far, far),
+        scratch_shapes=[vmem(3, 24, 32, 128), vmem(3, 24, 32, 128), vmem(3, 16, 16, 128), dma((2,))],
+        compiler_params=pltpu.CompilerParams(vmem_limit_bytes=16 << 20),
+    )(*inner)
 
 
 def solution(mesh):

time: 31.6 us -> 27.5 us (0.87)
  local copies, waits for them, and re-layouts: 4.99 us -> 0 us
  Pallas kernels: 25.8 us -> 26.8 us
    unnamed x10 -> x0, local copies, waits for them, and re-layouts: 4.99 us -> none
    pallas_call x1 -> x2, Pallas kernels: 25.8 us -> 26.8 us  [the longest x1 24.4 us: local(): pl.pallas_call(functools.partial(kernel, nx, ny), out_shape=(jax.ShapeDty...]
where the time goes in v2:
time: 27.5 us; the launch traced here: 27.4 us
  Pallas kernels  26.8 us (97%)
  between operations  0.64 us (2%)
    pallas_call x1, Pallas kernels, local(): pl.pallas_call(functools.partial(kernel, nx, ny), out_shape=(jax.ShapeDty...  24.4 us
    pallas_call x1, Pallas kernels, local(): pl.pallas_call(after, out_shape=(shape, shape), in_specs=[near] * 3, out_...  2.33 us

profile of v2, /device:TPU:121, one launch (start us, length us, event | category | flops | bytes accessed | tf_op | source)
XLA Modules:
  0.0 27.4 jit_solution(8598826075699083861)
XLA Ops:
  0.6 24.4 %shard_map.59 = (f32[3,24,32,128]{3,2,1,0:T(8,128)S(1)}, f32[4,24,32,128]{3,2,1,0:T(8,128)S(1)}, f32[16,16,128]{2,1,0:T(8,128)S(1)}) custom-call(f32[3,16,16,128]{3,2,1,0:T(8,128)} %load.1, f32[16,16,128]{2,1,0:T(8,128)} %modulus.1, f32[16,16,128]{2,1,0:T(8,128)} %anchor.1, s32[4,4,16]{2,1,0:T(4,128)} %wall_mask.1), custom_call_target="tpu_custom_call" | custom-call | tf_op jit(solution)/shard_map/pallas_call | solution.py:423
  25.1 2.3 %shard_map.60 = (f32[3,16,16,128]{3,2,1,0:T(8,128)}, f32[3,16,16,128]{3,2,1,0:T(8,128)}) custom-call(f32[3,24,32,128]{3,2,1,0:T(8,128)S(1)} %get-tuple-element.5.XC, f32[4,24,32,128]{3,2,1,0:T(8,128)S(1)} %get-tuple-element.6.BK, f32[16,16,128]{2,1,0:T(8,128)S(1)} %get-tuple-element.7.DG), custom_call_target="tpu_custom_call" | custom-call | tf_op jit(solution)/shard_map/pallas_call | solution.py:448

commit v3 on v2

--- a/solution.py
+++ b/solution.py
@@ -10,10 +10,10 @@
 COARSE_STEPS = 8
 MESH = pl.DeviceIdType.MESH
 
-NEAR = [(-1, 0), (1, 0), (0, -1), (0, 1), (-1, -1), (-1, 1), (1, -1), (1, 1)]
+NEAR = [(-1, -1), (-1, 1), (1, -1), (1, 1), (-1, 0), (1, 0), (0, -1), (0, 1)]
 FAR = [(-2, 0), (2, 0), (0, -2), (0, 2)]
 KNIGHT = [(s * a, t * b) for a, b in ((2, 1), (1, 2)) for s in (-1, 1) for t in (-1, 1)]
-ALL = NEAR + FAR + KNIGHT
+ALL = KNIGHT + FAR + NEAR
 
 
 def rates(low, high, steps):
@@ -28,23 +28,29 @@
     return theta, out
 
 
-def around(src, planes, rows, ends, fold):
-    x, (r0, n) = planes, rows
-    first, last = ends
-    v = src[0:3, x, r0 : r0 + n, :]
-    below = src[0:3, x - 1, r0 : r0 + n, :]
-    above = pltpu.roll(v, 64, 2) if fold else src[0:3, x + 1, r0 : r0 + n, :]
+def around(src, x, rows, ends, held, fold=False):
+    r0, n = rows
+    first, last = ends[n]
+
+    def plane(p):
+        if (p, rows) not in held:
+            held[p, rows] = src[0:3, p, r0 : r0 + n, :]
+        return held[p, rows]
+
+    below, v = plane(x - 1), plane(x)
+    above = pltpu.roll(v, 64, 2) if fold else plane(x + 1)
     nb = jnp.where(first, 0.0, pltpu.roll(v, 1, 2)) + jnp.where(last, 0.0, pltpu.roll(v, 127, 2))
     nb = nb + (below + above)
     nb = nb + (src[0:3, x, r0 - 1 : r0 + n - 1, :] + src[0:3, x, r0 + 1 : r0 + n + 1, :])
     return v, nb
 
 
-def sweep(dst, src, prev, rhs, stiff, coefs, planes, rows, ends, fold_at=None):
+def sweep(dst, src, prev, rhs, stiff, coefs, planes, rows_of, ends, fold_at=None):
     cv, cn, cb, cp = coefs
-    r0, n = rows
+    held = {}
     for x in planes:
-        v, nb = around(src, x, rows, ends, x == fold_at)
+        r0, n = rows_of(x)
+        v, nb = around(src, x, (r0, n), ends, held, x == fold_at)
         out = cv * v + (cn * stiff(x, r0, n))[None] * nb
         if cb:
             out = out + cb * rhs[0:3, x, r0 : r0 + n, :]
@@ -53,10 +59,28 @@
         dst[0:3, x, r0 : r0 + n, :] = out
 
 
+def lane_ends(period):
+    lane = lax.broadcasted_iota(jnp.int32, (3, 24, 128), 2) % period
+    first, last = lane == 0, lane == period - 1
+    return {24: (first, last), 16: (first[:, :16], last[:, :16])}
+
+
+def fine_rows(reach):
+    return lambda x: (8, 16) if x in (4 - reach, 19 + reach) else (4, 24)
+
+
+def coarse_rows(step):
+    def of(x):
+        away = max(0, 10 - x)
+        return (12, 16) if (11 - step - away if away else 10 - step) <= 4 else (8, 24)
+
+    return of
+
+
 def kernel(
     nx, ny, load, modulus, anchor, wall_mask, XC, BK, DG,
     f_load, f_mod, f_anc, mask, INV, XA, SY, RY, SC, RC, SPY, RPY, SPC, RPC,
-    ZC, LC, ZR, LH, IDC, PB, PK, Q, CB, CK, CX, CY, RB, RK, R2, RY2, RN, RM2, ZF,
+    ZC, LC, ZR, LH, IDC, PB, PK, Q, CB, CK, CX, CY, RB, RD, PC, RK, R2, RY2, RN, RM2, ZF,
     in_sem, s1, r1, sk, rk, s2, r2, sp, rp,
 ):
     ix, iy = lax.axis_index("gx"), lax.axis_index("gy")
@@ -138,7 +162,7 @@
         if abs(d[0]) < 2 and abs(d[1]) < 2:
             if d[0] == 0:
                 return CB.at[:, 10:14, 8:16, :] if d[1] < 0 else CB.at[:, 10:14, 24:32, :]
-            return RB.at[lo_hi(d[0]), d[1] + 1]
+            return RB.at[lo_hi(d[0])] if d[1] == 0 else RD.at[lo_hi(d[0]), lo_hi(d[1])]
         if d[1] == 0:
             return R2.at[lo_hi(d[0])]
         if d[0] == 0:
@@ -149,7 +173,7 @@
 
     def coarse_to(d):
         if abs(d[0]) < 2 and abs(d[1]) < 2:
-            return PB
+            return PB if d[0] == 0 or d[1] == 0 else PC.at[lo_hi(d[0]), lo_hi(d[1])]
         if d[1] == 0:
             return PB.at[:, 0]
         if d[0] == 0:
@@ -170,8 +194,10 @@
                 def _():
                     copy(k, d).start()
 
-        def wait():
+        def wait(chosen=lambda d: True):
             for k, d in enumerate(partners):
+                if not chosen(d):
+                    continue
 
                 @pl.when(there(opposite(d)))
                 def _():
@@ -262,35 +288,54 @@
     CK[10:14, 16:24, :] = coarse_k
     kay[0]()
 
-    lane = lax.broadcasted_iota(jnp.int32, (3, 24, 128), 2)
-    ends = (lane == 0, lane == 127)
-    short = (ends[0][:, :16], ends[1][:, :16])
+    ends = lane_ends(128)
     theta, ((a1, b1), (a2, b2)) = rates(0.5, 2.0, SMOOTH)
 
     def fine_k(x, r0, n):
         return BK[3, x, r0 : r0 + n, :]
 
-    one[1]()
+    def smooth(second, third, pairs):
+        coefs = ((1.0 + a1 - b1) / theta + b1, b1 / theta, 0.0, 0.0)
+        for planes in second:
+            sweep(XA, BK, None, BK, fine_k, coefs, planes, fine_rows(2), ends)
+        coefs = (1.0 + a2 - b2, b2, b2 - a2 / theta, 0.0)
+        for planes in third:
+            sweep(XC, XA, None, BK, fine_k, coefs, planes, fine_rows(1), ends)
+        held = {}
+        for c in pairs:
+            total = 0.0
+            for x in (4 + 2 * c, 5 + 2 * c):
+                v, nb = around(XC, x, (8, 16), ends, held)
+                total = total + DG[x - 4][None] * (BK[0:3, x, 8:24, :] - v + fine_k(x, 8, 16)[None] * nb)
+            ZR[:, c] = total
+
+    one[1](lambda d: d[0] == 0)
     for x in range(16):
         BK[:, 4 + x, 4:8, :] = RY[0, :, x]
         BK[:, 4 + x, 24:28, :] = RY[1, :, x]
+    smooth([range(5, 19)], [range(6, 18)], range(2, 6))
+    one[1](lambda d: d[0] != 0)
     for cx, x0 in ((0, 2), (1, 20)):
         BK[:, x0 : x0 + 2, 4:8, :] = RC[2 * cx]
         BK[:, x0 : x0 + 2, 24:28, :] = RC[2 * cx + 1]
-    wide = (4, 24)
-    sweep(XA, BK, None, BK, fine_k, ((1.0 + a1 - b1) / theta + b1, b1 / theta, 0.0, 0.0), range(2, 22), wide, ends)
-    sweep(XC, XA, None, BK, fine_k, (1.0 + a2 - b2, b2, b2 - a2 / theta, 0.0), range(3, 21), wide, ends)
-
-    for c in range(8):
-        total = 0.0
-        for x in (4 + 2 * c, 5 + 2 * c):
-            v, nb = around(XC, x, (8, 16), short, False)
-            total = total + DG[x - 4][None] * (BK[0:3, x, 8:24, :] - v + fine_k(x, 8, 16)[None] * nb)
-        ZR[:, c] = total
+    smooth([range(2, 5), range(19, 22)], [range(3, 6), range(18, 21)], (0, 1, 6, 7))
+
     for f in range(3):
         gather_pairs(ZR, LH, f)
     rest = boxes(LH, 3).reshape(3, 4, 8, 128) * IDC[...][None]
     PB[...] = rest
+    left = lax.broadcasted_iota(jnp.int32, (8, 128), 1) < 64
+    row = lax.broadcasted_iota(jnp.int32, (8, 128), 0)
+    for dx in (0, 1):
+        far_half = left if dx else jnp.logical_not(left)
+        first_two = jnp.where(far_half, pltpu.roll(rest[:, 1], 64, 2), rest[:, 0])
+        last_two = jnp.where(far_half, pltpu.roll(rest[:, 3], 64, 2), rest[:, 2])
+        for dy, shift1, shift0, has1, has0 in ((0, 5, 6, row >= 5, row >= 6), (1, 3, 2, row < 3, row < 2)):
+            odd = jnp.where(has1, pltpu.roll(rest[:, 1], shift1, 1), rest[:, 3])
+            even = jnp.where(has0, pltpu.roll(rest[:, 0], shift0, 1), rest[:, 2])
+            PC[dx, dy, 0] = first_two
+            PC[dx, dy, 1] = last_two
+            PC[dx, dy, 2] = jnp.where(far_half, odd, pltpu.roll(even, 64, 2))
     for j in range(4):
         Q[0, j, 0:3] = rest[:, j, 0, :]
         Q[1, j, 0:3] = rest[:, j, 7, :]
@@ -304,8 +349,6 @@
         SPC[2 * cx] = XC[:, x0 : x0 + 3, 8:12, :]
         SPC[2 * cx + 1] = XC[:, x0 : x0 + 3, 20:24, :]
     pre[0]()
-
-    left = lax.broadcasted_iota(jnp.int32, (8, 128), 1) < 64
 
     def meet(lo, hi):
         return pltpu.roll(jnp.where(left[: lo.shape[-2]], hi, lo), 64, lo.ndim - 1)
@@ -318,13 +361,20 @@
             CK[2 + j, rows, :] = jnp.where(left, lo, hi)
             CK[9 - j, rows, :] = meet(lo, hi)
     two[1]()
-    for y in range(3):
-        rows = slice(8 + 8 * y, 16 + 8 * y)
-        for j in range(4):
-            for f in range(3):
-                lo, hi = RB[0, y, f, j], RB[1, y, f, j]
-                CB[f, 2 + j, rows, :] = jnp.where(left, lo, hi)
-                CB[f, 9 - j, rows, :] = meet(lo, hi)
+    for j in range(4):
+        lo, hi = RB[0, :, j], RB[1, :, j]
+        CB[:, 2 + j, 16:24, :] = jnp.where(left, lo, hi)
+        CB[:, 9 - j, 16:24, :] = meet(lo, hi)
+    for y, rows, back1, back0 in ((0, slice(8, 16), 5, 6), (1, slice(24, 32), 3, 2)):
+        for part in (0, 1):
+            lo, hi = RD[0, y, part], RD[1, y, part]
+            CB[:, 9 - 2 * part, rows, :] = meet(lo, hi)
+            CB[:, 8 - 2 * part, rows, :] = jnp.where(left, lo, hi)
+        odd, even = jnp.where(left, RD[0, y, 2], RD[1, y, 2]), meet(RD[0, y, 2], RD[1, y, 2])
+        CB[:, 5, rows, :] = odd
+        CB[:, 3, rows, :] = pltpu.roll(odd, back1, 1)
+        CB[:, 4, rows, :] = even
+        CB[:, 2, rows, :] = pltpu.roll(even, back0, 1)
     for f in range(3):
         CB[f, 1, 16:24, :] = meet(R2[0, f], R2[1, f])
     for y, near, far in ((0, 15, 7), (1, 24, 32)):
@@ -336,9 +386,7 @@
             for j in range(4):
                 CB[f, 10 + j, far : far + 1, :] = RY2[y, j, f : f + 1]
 
-    lane = lane % 64
-    ends_c = (lane == 0, lane == 63)
-    short_c = (ends_c[0][:, :16], ends_c[1][:, :16])
+    ends_c = lane_ends(64)
     theta_c, steps = rates(0.05, 2.0, COARSE_STEPS)
 
     def coarse_k_at(x, r0, n):
@@ -347,7 +395,6 @@
     at = CB
     for t in range(2, COARSE_STEPS + 1):
         a, b = steps[t - 2]
-        rows, e = ((8, 24), ends_c) if t < 6 else ((12, 16), short_c)
         to = CY if t % 2 == 0 else CX
         if t == 2:
             coefs, prev = ((1.0 + a - b) / theta_c + b, b / theta_c, 0.0, 0.0), None
@@ -355,7 +402,7 @@
             coefs, prev = (1.0 + a - b, b, b - a / theta_c, 0.0), None
         else:
             coefs, prev = (1.0 + a - b, b, b, -a), to
-        sweep(to, at, prev, CB, coarse_k_at, coefs, range(t, 14), rows, e, 13)
+        sweep(to, at, prev, CB, coarse_k_at, coefs, range(t, 14), coarse_rows(t), ends_c, 13)
         at = to
 
     repeat = (
@@ -386,25 +433,23 @@
 
 
 def after(XC, BK, DG, out_sol, out_rem, XA, XB, RM, out_sem):
-    lane = lax.broadcasted_iota(jnp.int32, (3, 24, 128), 2)
-    ends = (lane == 0, lane == 127)
-    short = (ends[0][:, :16], ends[1][:, :16])
+    ends = lane_ends(128)
     theta, ((a1, b1), (a2, b2)) = rates(0.5, 2.0, SMOOTH)
-    wide = (4, 24)
 
     def fine_k(x, r0, n):
         return BK[3, x, r0 : r0 + n, :]
 
-    sweep(XA, XC, None, BK, fine_k, (1.0 - 1.0 / theta, 1.0 / theta, 1.0 / theta, 0.0), range(1, 23), wide, ends)
-    sweep(XB, XA, XC, BK, fine_k, (1.0 + a1 - b1, b1, b1, -a1), range(2, 22), wide, ends)
-    sweep(XA, XB, XA, BK, fine_k, (1.0 + a2 - b2, b2, b2, -a2), range(3, 21), wide, ends)
+    sweep(XA, XC, None, BK, fine_k, (1.0 - 1.0 / theta, 1.0 / theta, 1.0 / theta, 0.0), range(1, 23), fine_rows(3), ends)
+    sweep(XB, XA, XC, BK, fine_k, (1.0 + a1 - b1, b1, b1, -a1), range(2, 22), fine_rows(2), ends)
+    sweep(XA, XB, XA, BK, fine_k, (1.0 + a2 - b2, b2, b2, -a2), range(3, 21), fine_rows(1), ends)
     put = [
         pltpu.make_async_copy(XA.at[:, 4:20, 8:24, :], out_sol, out_sem.at[0]),
         pltpu.make_async_copy(RM, out_rem, out_sem.at[1]),
     ]
     put[0].start()
+    held = {}
     for x in range(4, 20):
-        v, nb = around(XA, x, (8, 16), short, False)
+        v, nb = around(XA, x, (8, 16), ends, held)
         RM[:, x - 4] = DG[x - 4][None] * (BK[0:3, x, 8:24, :] - v + fine_k(x, 8, 16)[None] * nb)
     put[1].start()
     put[0].wait()
@@ -437,7 +482,8 @@
             vmem(2, 8, 16, 128), vmem(2, 4, 8, 256), vmem(3, 8, 16, 128), vmem(3, 4, 8, 256),
             vmem(4, 8, 128), vmem(3, 4, 8, 128), vmem(4, 8, 128), vmem(2, 4, 4, 128),
             vmem(3, 14, 40, 128), vmem(14, 40, 128), vmem(3, 14, 40, 128), vmem(3, 14, 40, 128),
-            vmem(2, 3, 3, 4, 8, 128), vmem(2, 3, 4, 8, 128), vmem(2, 3, 8, 128),
+            vmem(2, 3, 4, 8, 128), vmem(2, 2, 3, 3, 8, 128), vmem(2, 2, 3, 3, 8, 128),
+            vmem(2, 3, 4, 8, 128), vmem(2, 3, 8, 128),
             vmem(2, 4, 4, 128), vmem(2, 2, 4, 128), vmem(2, 2, 4, 128),
             vmem(3, 6, 24, 128),
             dma((4,)), dma((8,)), dma((8,)), dma((8,)), dma((8,)), dma((20,)), dma((20,)), dma((8,)), dma((8,)),

time: 27.5 us -> 24.8 us (0.902); the launches traced: 27.4 us -> 24.4 us
  Pallas kernels: 26.8 us -> 23.7 us
    pallas_call x1, Pallas kernels: 24.4 us -> 21.5 us  [local(): pl.pallas_call(functools.partial(kernel, nx, ny), out_shape=(jax.ShapeDty...]
where the time goes in v3:
time: 24.8 us; the launch traced here: 24.4 us
  Pallas kernels  23.7 us (96%)
  between operations  0.64 us (3%)
    pallas_call x1, Pallas kernels, local(): pl.pallas_call(functools.partial(kernel, nx, ny), out_shape=(jax.ShapeDty...  21.5 us
    pallas_call x1, Pallas kernels, local(): pl.pallas_call(after, out_shape=(shape, shape), in_specs=[near] * 3, out_...  2.26 us

profile of v3, /device:TPU:121, one launch (start us, length us, event | category | flops | bytes accessed | tf_op | source)
XLA Modules:
  0.0 24.4 jit_solution(10380872609633004173)
XLA Ops:
  0.6 21.5 %shard_map.59 = (f32[3,24,32,128]{3,2,1,0:T(8,128)S(1)}, f32[4,24,32,128]{3,2,1,0:T(8,128)S(1)}, f32[16,16,128]{2,1,0:T(8,128)S(1)}) custom-call(f32[3,16,16,128]{3,2,1,0:T(8,128)} %load.1, f32[16,16,128]{2,1,0:T(8,128)} %modulus.1, f32[16,16,128]{2,1,0:T(8,128)} %anchor.1, s32[4,4,16]{2,1,0:T(4,128)} %wall_mask.1), custom_call_target="tpu_custom_call" | custom-call | tf_op jit(solution)/shard_map/pallas_call | solution.py:468
  22.1 2.3 %shard_map.60 = (f32[3,16,16,128]{3,2,1,0:T(8,128)}, f32[3,16,16,128]{3,2,1,0:T(8,128)}) custom-call(f32[3,24,32,128]{3,2,1,0:T(8,128)S(1)} %get-tuple-element.5.XC, f32[4,24,32,128]{3,2,1,0:T(8,128)S(1)} %get-tuple-element.6.BK, f32[16,16,128]{2,1,0:T(8,128)S(1)} %get-tuple-element.7.DG), custom_call_target="tpu_custom_call" | custom-call | tf_op jit(solution)/shard_map/pallas_call | solution.py:494

commit v4 on v3

--- a/solution.py
+++ b/solution.py
@@ -104,7 +104,7 @@
         return (-d[0], -d[1])
 
     barrier = pltpu.get_barrier_semaphore()
-    for d in ALL:
+    for d in NEAR:
 
         @pl.when(there(d))
         def _():
@@ -255,7 +255,7 @@
         SC[2 * cx] = BK[:, x0 : x0 + 2, 8:12, :]
         SC[2 * cx + 1] = BK[:, x0 : x0 + 2, 20:24, :]
 
-    pl.semaphore_wait(barrier, sum(there(d).astype(jnp.int32) for d in ALL))
+    pl.semaphore_wait(barrier, sum(there(d).astype(jnp.int32) for d in NEAR))
     one[0]()
 
     pair_sum = 0.125 * (

time: 24.8 us -> 23.3 us (0.940)
  Pallas kernels: 23.7 us -> 22.4 us
    pallas_call x1, Pallas kernels: 21.5 us -> 20.2 us  [local(): pl.pallas_call(functools.partial(kernel, nx, ny), out_shape=(jax.ShapeDty...]
where the time goes in v4:
time: 23.3 us; the launch traced here: 23.1 us
  Pallas kernels  22.4 us (96%)
  between operations  0.64 us (3%)
    pallas_call x1, Pallas kernels, local(): pl.pallas_call(functools.partial(kernel, nx, ny), out_shape=(jax.ShapeDty...  20.2 us
    pallas_call x1, Pallas kernels, local(): pl.pallas_call(after, out_shape=(shape, shape), in_specs=[near] * 3, out_...  2.26 us

profile of v4, /device:TPU:121, one launch (start us, length us, event | category | flops | bytes accessed | tf_op | source)
XLA Modules:
  0.0 23.1 jit_solution(3675900968283761045)
XLA Ops:
  0.6 20.2 %shard_map.59 = (f32[3,24,32,128]{3,2,1,0:T(8,128)S(1)}, f32[4,24,32,128]{3,2,1,0:T(8,128)S(1)}, f32[16,16,128]{2,1,0:T(8,128)S(1)}) custom-call(f32[3,16,16,128]{3,2,1,0:T(8,128)} %load.1, f32[16,16,128]{2,1,0:T(8,128)} %modulus.1, f32[16,16,128]{2,1,0:T(8,128)} %anchor.1, s32[4,4,16]{2,1,0:T(4,128)} %wall_mask.1), custom_call_target="tpu_custom_call" | custom-call | tf_op jit(solution)/shard_map/pallas_call | solution.py:468
  20.8 2.3 %shard_map.60 = (f32[3,16,16,128]{3,2,1,0:T(8,128)}, f32[3,16,16,128]{3,2,1,0:T(8,128)}) custom-call(f32[3,24,32,128]{3,2,1,0:T(8,128)S(1)} %get-tuple-element.5.XC, f32[4,24,32,128]{3,2,1,0:T(8,128)S(1)} %get-tuple-element.6.BK, f32[16,16,128]{2,1,0:T(8,128)S(1)} %get-tuple-element.7.DG), custom_call_target="tpu_custom_call" | custom-call | tf_op jit(solution)/shard_map/pallas_call | solution.py:494

commit v5 on v4

--- a/solution.py
+++ b/solution.py
@@ -13,7 +13,7 @@
 NEAR = [(-1, -1), (-1, 1), (1, -1), (1, 1), (-1, 0), (1, 0), (0, -1), (0, 1)]
 FAR = [(-2, 0), (2, 0), (0, -2), (0, 2)]
 KNIGHT = [(s * a, t * b) for a, b in ((2, 1), (1, 2)) for s in (-1, 1) for t in (-1, 1)]
-ALL = KNIGHT + FAR + NEAR
+ALL = KNIGHT + FAR + NEAR[4:6] + NEAR[:4] + NEAR[6:]
 
 
 def rates(low, high, steps):
@@ -407,7 +407,7 @@
 
     repeat = (
         lax.broadcasted_iota(jnp.int32, (128, 256), 1) // 2 == lax.broadcasted_iota(jnp.int32, (128, 256), 0)
-    ).astype(jnp.float32)
+    ).astype(jnp.bfloat16)
     pre[1]()
     pre[2]()
     for x in range(16):
@@ -421,9 +421,13 @@
             v = at[f, 8 + i, 14:26, :]
             ZF[f, i, pl.ds(0, 12, 2), :] = v
             ZF[f, i, pl.ds(1, 12, 2), :] = v
-        up = jnp.dot(
-            ZF[f].reshape(144, 128), repeat, precision=lax.Precision.HIGHEST, preferred_element_type=jnp.float32
-        ).reshape(6, 24, 256)
+        whole = ZF[f].reshape(144, 128)
+        up = 0.0
+        for _ in range(3):
+            piece = whole.astype(jnp.bfloat16)
+            up = up + jnp.dot(piece, repeat, preferred_element_type=jnp.float32)
+            whole = whole - piece.astype(jnp.float32)
+        up = up.reshape(6, 24, 256)
         for i in range(6):
             for x, v in ((2 * i, up[i, :, 0:128]), (22 - 2 * i, up[i, :, 128:256])):
                 XC[f, x, 4:28, :] = XC[f, x, 4:28, :] + v
@@ -444,16 +448,20 @@
     sweep(XA, XB, XA, BK, fine_k, (1.0 + a2 - b2, b2, b2, -a2), range(3, 21), fine_rows(1), ends)
     put = [
         pltpu.make_async_copy(XA.at[:, 4:20, 8:24, :], out_sol, out_sem.at[0]),
-        pltpu.make_async_copy(RM, out_rem, out_sem.at[1]),
+        *(
+            pltpu.make_async_copy(RM.at[:, a : a + 4], out_rem.at[:, a : a + 4], out_sem.at[1 + a // 4])
+            for a in range(0, 16, 4)
+        ),
     ]
     put[0].start()
     held = {}
     for x in range(4, 20):
         v, nb = around(XA, x, (8, 16), ends, held)
         RM[:, x - 4] = DG[x - 4][None] * (BK[0:3, x, 8:24, :] - v + fine_k(x, 8, 16)[None] * nb)
-    put[1].start()
-    put[0].wait()
-    put[1].wait()
+        if x % 4 == 3:
+            put[x // 4].start()
+    for copy in put:
+        copy.wait()
 
 
 def local(nx, ny, load, modulus, anchor, wall_mask):
@@ -496,7 +504,7 @@
         out_shape=(shape, shape),
         in_specs=[near] * 3,
         out_specs=(far, far),
-        scratch_shapes=[vmem(3, 24, 32, 128), vmem(3, 24, 32, 128), vmem(3, 16, 16, 128), dma((2,))],
+        scratch_shapes=[vmem(3, 24, 32, 128), vmem(3, 24, 32, 128), vmem(3, 16, 16, 128), dma((5,))],
         compiler_params=pltpu.CompilerParams(vmem_limit_bytes=16 << 20),
     )(*inner)
 

time: 23.3 us -> 22.9 us (0.983)
  no operation moved by 1% of the time
where the time goes in v5:
time: 22.9 us; the launch traced here: 22.8 us
  Pallas kernels  22.2 us (97%)
  between operations  0.64 us (3%)
    pallas_call x1, Pallas kernels, local(): pl.pallas_call(functools.partial(kernel, nx, ny), out_shape=(jax.ShapeDty...  20 us
    pallas_call x1, Pallas kernels, local(): pl.pallas_call(after, out_shape=(shape, shape), in_specs=[near] * 3, out_...  2.18 us

profile of v5, /device:TPU:121, one launch (start us, length us, event | category | flops | bytes accessed | tf_op | source)
XLA Modules:
  0.0 22.8 jit_solution(15413682341421940441)
XLA Ops:
  0.6 20.0 %shard_map.59 = (f32[3,24,32,128]{3,2,1,0:T(8,128)S(1)}, f32[4,24,32,128]{3,2,1,0:T(8,128)S(1)}, f32[16,16,128]{2,1,0:T(8,128)S(1)}) custom-call(f32[3,16,16,128]{3,2,1,0:T(8,128)} %load.1, f32[16,16,128]{2,1,0:T(8,128)} %modulus.1, f32[16,16,128]{2,1,0:T(8,128)} %anchor.1, s32[4,4,16]{2,1,0:T(4,128)} %wall_mask.1), custom_call_target="tpu_custom_call" | custom-call | tf_op jit(solution)/shard_map/pallas_call | solution.py:476
  20.6 2.2 %shard_map.60 = (f32[3,16,16,128]{3,2,1,0:T(8,128)}, f32[3,16,16,128]{3,2,1,0:T(8,128)}) custom-call(f32[3,24,32,128]{3,2,1,0:T(8,128)S(1)} %get-tuple-element.5.XC, f32[4,24,32,128]{3,2,1,0:T(8,128)S(1)} %get-tuple-element.6.BK, f32[16,16,128]{2,1,0:T(8,128)S(1)} %get-tuple-element.7.DG), custom_call_target="tpu_custom_call" | custom-call | tf_op jit(solution)/shard_map/pallas_call | solution.py:502

commit v6 on v5

--- a/solution.py
+++ b/solution.py
@@ -81,7 +81,7 @@
     nx, ny, load, modulus, anchor, wall_mask, XC, BK, DG,
     f_load, f_mod, f_anc, mask, INV, XA, SY, RY, SC, RC, SPY, RPY, SPC, RPC,
     ZC, LC, ZR, LH, IDC, PB, PK, Q, CB, CK, CX, CY, RB, RD, PC, RK, R2, RY2, RN, RM2, ZF,
-    in_sem, s1, r1, sk, rk, s2, r2, sp, rp,
+    in_sem, s1, r1, sk, rk, s2, r2, sp, rp, s3, r3,
 ):
     ix, iy = lax.axis_index("gx"), lax.axis_index("gy")
 
@@ -162,7 +162,7 @@
         if abs(d[0]) < 2 and abs(d[1]) < 2:
             if d[0] == 0:
                 return CB.at[:, 10:14, 8:16, :] if d[1] < 0 else CB.at[:, 10:14, 24:32, :]
-            return RB.at[lo_hi(d[0])] if d[1] == 0 else RD.at[lo_hi(d[0]), lo_hi(d[1])]
+            return RB.at[lo_hi(d[0])] if d[1] == 0 else RD.at[lo_hi(d[0]), lo_hi(d[1]), 0:2]
         if d[1] == 0:
             return R2.at[lo_hi(d[0])]
         if d[0] == 0:
@@ -173,12 +173,18 @@
 
     def coarse_to(d):
         if abs(d[0]) < 2 and abs(d[1]) < 2:
-            return PB if d[0] == 0 or d[1] == 0 else PC.at[lo_hi(d[0]), lo_hi(d[1])]
+            return PB if d[0] == 0 or d[1] == 0 else PC.at[lo_hi(d[0]), lo_hi(d[1]), 0:2]
         if d[1] == 0:
             return PB.at[:, 0]
         if d[0] == 0:
             return Q.at[lo_hi(d[1])]
         return Q.at[lo_hi(d[1]), 0]
+
+    def early_from(d):
+        return RD.at[lo_hi(d[0]), lo_hi(d[1]), 2]
+
+    def early_to(d):
+        return PC.at[lo_hi(d[0]), lo_hi(d[1]), 2]
 
     def exchange(partners, to, came, send, recv):
         def copy(k, d):
@@ -216,8 +222,9 @@
     pre = exchange(NEAR, pre_to, pre_from, sp, rp)
     kay = exchange(NEAR, stiff_to, stiff_from, sk, rk)
     two = exchange(ALL, coarse_to, coarse_from, s2, r2)
-
-    for partners, came in ((NEAR, first_from), (NEAR, pre_from), (NEAR, stiff_from), (ALL, coarse_from)):
+    early = exchange(NEAR[:4], early_to, early_from, s3, r3)
+
+    for partners, came in ((NEAR, first_from), (NEAR, pre_from), (NEAR, stiff_from), (ALL, coarse_from), (NEAR[:4], early_from)):
         for d in partners:
 
             @pl.when(jnp.logical_not(there(d)))
@@ -262,16 +269,16 @@
         lax.broadcasted_iota(jnp.int32, (256, 128), 0) // 2 == lax.broadcasted_iota(jnp.int32, (256, 128), 1)
     ).astype(jnp.float32)
 
-    def gather_pairs(place, lhs, f):
-        for c in range(8):
+    def gather_pairs(place, lhs, f, cells=range(8)):
+        for c in cells:
             v = place[f, c, pl.ds(0, 8, 2), :] + place[f, c, pl.ds(1, 8, 2), :]
             if c < 4:
                 lhs[f, c, :, 0:128] = v
             else:
                 lhs[f, 7 - c, :, 128:256] = v
 
-    def boxes(lhs, count):
-        flat = lhs[...].reshape(count * 32, 256)
+    def boxes(lhs):
+        flat = lhs.reshape(-1, 256)
         return jnp.dot(flat, pair_sum, precision=lax.Precision.HIGHEST, preferred_element_type=jnp.float32)
 
     for c in range(8):
@@ -279,7 +286,7 @@
         ZC[1, c] = f_anc[2 * c] + f_anc[2 * c + 1]
     gather_pairs(ZC, LC, 0)
     gather_pairs(ZC, LC, 1)
-    means = boxes(LC, 2)
+    means = boxes(LC[...])
     coarse_stiff = 0.25 * means[0:32]
     inv = 1.0 / (means[32:64] + 6.0 * coarse_stiff)
     IDC[...] = inv.reshape(4, 8, 128)
@@ -314,6 +321,17 @@
         BK[:, 4 + x, 4:8, :] = RY[0, :, x]
         BK[:, 4 + x, 24:28, :] = RY[1, :, x]
     smooth([range(5, 19)], [range(6, 18)], range(2, 6))
+    left = lax.broadcasted_iota(jnp.int32, (8, 128), 1) < 64
+    row = lax.broadcasted_iota(jnp.int32, (8, 128), 0)
+    for f in range(3):
+        gather_pairs(ZR, LH, f, range(2, 6))
+    inner = boxes(LH[:, 2:4]).reshape(3, 2, 8, 128) * IDC[2:4][None]
+    PB[:, 2:4] = inner
+    for dx in (0, 1):
+        far_half = left if dx else jnp.logical_not(left)
+        for dy in (0, 1):
+            PC[dx, dy, 2] = jnp.where(far_half, pltpu.roll(inner[:, 1], 64, 2), inner[:, 0])
+    early[0]()
     one[1](lambda d: d[0] != 0)
     for cx, x0 in ((0, 2), (1, 20)):
         BK[:, x0 : x0 + 2, 4:8, :] = RC[2 * cx]
@@ -321,26 +339,23 @@
     smooth([range(2, 5), range(19, 22)], [range(3, 6), range(18, 21)], (0, 1, 6, 7))
 
     for f in range(3):
-        gather_pairs(ZR, LH, f)
-    rest = boxes(LH, 3).reshape(3, 4, 8, 128) * IDC[...][None]
-    PB[...] = rest
-    left = lax.broadcasted_iota(jnp.int32, (8, 128), 1) < 64
-    row = lax.broadcasted_iota(jnp.int32, (8, 128), 0)
+        gather_pairs(ZR, LH, f, (0, 1, 6, 7))
+    outer = boxes(LH[:, 0:2]).reshape(3, 2, 8, 128) * IDC[0:2][None]
+    PB[:, 0:2] = outer
+    rest = [outer[:, 0], outer[:, 1], inner[:, 0], inner[:, 1]]
     for dx in (0, 1):
         far_half = left if dx else jnp.logical_not(left)
-        first_two = jnp.where(far_half, pltpu.roll(rest[:, 1], 64, 2), rest[:, 0])
-        last_two = jnp.where(far_half, pltpu.roll(rest[:, 3], 64, 2), rest[:, 2])
+        first_two = jnp.where(far_half, pltpu.roll(rest[1], 64, 2), rest[0])
         for dy, shift1, shift0, has1, has0 in ((0, 5, 6, row >= 5, row >= 6), (1, 3, 2, row < 3, row < 2)):
-            odd = jnp.where(has1, pltpu.roll(rest[:, 1], shift1, 1), rest[:, 3])
-            even = jnp.where(has0, pltpu.roll(rest[:, 0], shift0, 1), rest[:, 2])
+            odd = jnp.where(has1, pltpu.roll(rest[1], shift1, 1), rest[3])
+            even = jnp.where(has0, pltpu.roll(rest[0], shift0, 1), rest[2])
             PC[dx, dy, 0] = first_two
-            PC[dx, dy, 1] = last_two
-            PC[dx, dy, 2] = jnp.where(far_half, odd, pltpu.roll(even, 64, 2))
+            PC[dx, dy, 1] = jnp.where(far_half, odd, pltpu.roll(even, 64, 2))
     for j in range(4):
-        Q[0, j, 0:3] = rest[:, j, 0, :]
-        Q[1, j, 0:3] = rest[:, j, 7, :]
+        Q[0, j, 0:3] = rest[j][:, 0, :]
+        Q[1, j, 0:3] = rest[j][:, 7, :]
     two[0]()
-    CB[:, 10:14, 16:24, :] = rest
+    CB[:, 10:14, 16:24, :] = PB[...]
 
     for x in range(16):
         SPY[0, :, x] = XC[:, 4 + x, 8:12, :]
@@ -360,6 +375,7 @@
             lo, hi = RK[0, y, j], RK[1, y, j]
             CK[2 + j, rows, :] = jnp.where(left, lo, hi)
             CK[9 - j, rows, :] = meet(lo, hi)
+    early[1]()
     two[1]()
     for j in range(4):
         lo, hi = RB[0, :, j], RB[1, :, j]
@@ -367,10 +383,10 @@
         CB[:, 9 - j, 16:24, :] = meet(lo, hi)
     for y, rows, back1, back0 in ((0, slice(8, 16), 5, 6), (1, slice(24, 32), 3, 2)):
         for part in (0, 1):
-            lo, hi = RD[0, y, part], RD[1, y, part]
+            lo, hi = RD[0, y, 2 * part], RD[1, y, 2 * part]
             CB[:, 9 - 2 * part, rows, :] = meet(lo, hi)
             CB[:, 8 - 2 * part, rows, :] = jnp.where(left, lo, hi)
-        odd, even = jnp.where(left, RD[0, y, 2], RD[1, y, 2]), meet(RD[0, y, 2], RD[1, y, 2])
+        odd, even = jnp.where(left, RD[0, y, 1], RD[1, y, 1]), meet(RD[0, y, 1], RD[1, y, 1])
         CB[:, 5, rows, :] = odd
         CB[:, 3, rows, :] = pltpu.roll(odd, back1, 1)
         CB[:, 4, rows, :] = even
@@ -432,7 +448,7 @@
             for x, v in ((2 * i, up[i, :, 0:128]), (22 - 2 * i, up[i, :, 128:256])):
                 XC[f, x, 4:28, :] = XC[f, x, 4:28, :] + v
                 XC[f, x + 1, 4:28, :] = XC[f, x + 1, 4:28, :] + v
-    for _, _, drain in (one, kay, two):
+    for _, _, drain in (one, kay, early, two):
         drain()
 
 
@@ -494,7 +510,7 @@
             vmem(2, 3, 4, 8, 128), vmem(2, 3, 8, 128),
             vmem(2, 4, 4, 128), vmem(2, 2, 4, 128), vmem(2, 2, 4, 128),
             vmem(3, 6, 24, 128),
-            dma((4,)), dma((8,)), dma((8,)), dma((8,)), dma((8,)), dma((20,)), dma((20,)), dma((8,)), dma((8,)),
+            dma((4,)), dma((8,)), dma((8,)), dma((8,)), dma((8,)), dma((20,)), dma((20,)), dma((8,)), dma((8,)), dma((4,)), dma((4,)),
         ],
         compiler_params=pltpu.CompilerParams(collective_id=0, has_side_effects=True, vmem_limit_bytes=24 << 20),
     )(*(pltpu.with_memory_space_constraint(a, pltpu.HBM) for a in (load, modulus, anchor, wall_mask)))

time: 22.9 us -> 22.7 us (level)
  no operation moved by 1% of the time
where the time goes in v6:
time: 22.7 us; the launch traced here: 22.6 us
  Pallas kernels  22 us (97%)
  between operations  0.64 us (3%)
    pallas_call x1, Pallas kernels, local(): pl.pallas_call(functools.partial(kernel, nx, ny), out_shape=(jax.ShapeDty...  19.8 us
    pallas_call x1, Pallas kernels, local(): pl.pallas_call(after, out_shape=(shape, shape), in_specs=[near] * 3, out_...  2.18 us

profile of v6, /device:TPU:121, one launch (start us, length us, event | category | flops | bytes accessed | tf_op | source)
XLA Modules:
  0.0 22.6 jit_solution(18261155455622987929)
XLA Ops:
  0.6 19.8 %shard_map.59 = (f32[3,24,32,128]{3,2,1,0:T(8,128)S(1)}, f32[4,24,32,128]{3,2,1,0:T(8,128)S(1)}, f32[16,16,128]{2,1,0:T(8,128)S(1)}) custom-call(f32[3,16,16,128]{3,2,1,0:T(8,128)} %load.1, f32[16,16,128]{2,1,0:T(8,128)} %modulus.1, f32[16,16,128]{2,1,0:T(8,128)} %anchor.1, s32[4,4,16]{2,1,0:T(4,128)} %wall_mask.1), custom_call_target="tpu_custom_call" | custom-call | tf_op jit(solution)/shard_map/pallas_call | solution.py:492
  20.4 2.2 %shard_map.60 = (f32[3,16,16,128]{3,2,1,0:T(8,128)}, f32[3,16,16,128]{3,2,1,0:T(8,128)}) custom-call(f32[3,24,32,128]{3,2,1,0:T(8,128)S(1)} %get-tuple-element.5.XC, f32[4,24,32,128]{3,2,1,0:T(8,128)S(1)} %get-tuple-element.6.BK, f32[16,16,128]{2,1,0:T(8,128)S(1)} %get-tuple-element.7.DG), custom_call_target="tpu_custom_call" | custom-call | tf_op jit(solution)/shard_map/pallas_call | solution.py:518

commit v7 on v6

--- a/solution.py
+++ b/solution.py
@@ -51,9 +51,12 @@
     for x in planes:
         r0, n = rows_of(x)
         v, nb = around(src, x, (r0, n), ends, held, x == fold_at)
-        out = cv * v + (cn * stiff(x, r0, n))[None] * nb
-        if cb:
-            out = out + cb * rhs[0:3, x, r0 : r0 + n, :]
+        if cn == cb:
+            out = cv * v + cb * (rhs[0:3, x, r0 : r0 + n, :] + stiff(x, r0, n)[None] * nb)
+        else:
+            out = cv * v + (cn * stiff(x, r0, n))[None] * nb
+            if cb:
+                out = out + cb * rhs[0:3, x, r0 : r0 + n, :]
         if prev is not None:
             out = out + cp * prev[0:3, x, r0 : r0 + n, :]
         dst[0:3, x, r0 : r0 + n, :] = out

time: 22.7 us -> 22.7 us (level)
  no operation moved by 1% of the time
where the time goes in v7:
time: 22.7 us; the launch traced here: 22.6 us
  Pallas kernels  21.9 us (96%)
  between operations  0.64 us (3%)
    pallas_call x1, Pallas kernels, local(): pl.pallas_call(functools.partial(kernel, nx, ny), out_shape=(jax.ShapeDty...  19.8 us
    pallas_call x1, Pallas kernels, local(): pl.pallas_call(after, out_shape=(shape, shape), in_specs=[near] * 3, out_...  2.14 us

profile of v7, /device:TPU:121, one launch (start us, length us, event | category | flops | bytes accessed | tf_op | source)
XLA Modules:
  0.0 22.6 jit_solution(13313541070873237499)
XLA Ops:
  0.6 19.8 %shard_map.59 = (f32[3,24,32,128]{3,2,1,0:T(8,128)S(1)}, f32[4,24,32,128]{3,2,1,0:T(8,128)S(1)}, f32[16,16,128]{2,1,0:T(8,128)S(1)}) custom-call(f32[3,16,16,128]{3,2,1,0:T(8,128)} %load.1, f32[16,16,128]{2,1,0:T(8,128)} %modulus.1, f32[16,16,128]{2,1,0:T(8,128)} %anchor.1, s32[4,4,16]{2,1,0:T(4,128)} %wall_mask.1), custom_call_target="tpu_custom_call" | custom-call | tf_op jit(solution)/shard_map/pallas_call | solution.py:495
  20.4 2.1 %shard_map.60 = (f32[3,16,16,128]{3,2,1,0:T(8,128)}, f32[3,16,16,128]{3,2,1,0:T(8,128)}) custom-call(f32[3,24,32,128]{3,2,1,0:T(8,128)S(1)} %get-tuple-element.5.XC, f32[4,24,32,128]{3,2,1,0:T(8,128)S(1)} %get-tuple-element.6.BK, f32[16,16,128]{2,1,0:T(8,128)S(1)} %get-tuple-element.7.DG), custom_call_target="tpu_custom_call" | custom-call | tf_op jit(solution)/shard_map/pallas_call | solution.py:521
